TPU v7x, 32 devices: a whole 2x2x4 slice. The times are simulated.
32 devices in a mesh: ctx: 8 (over y, x, core), fsdp: 4 (over z).
Axes of the slice: x: 2, y: 2, z: 4, core: 2. Of those that a mesh axis runs over, the one named last changes fastest.
Arguments:
- states: bfloat16 [4, 3072, 1024], P('fsdp', 'ctx'), may hold values from -6 to 6
- norm_gain: float32 [512], replicated, may hold values from 0.1 to 1.9
- in_proj: bfloat16 [1024, 512], P('fsdp'), may hold values from -0.25 to 0.25
- conv_taps: float32 [2, 7, 1024], replicated, may hold values from -2 to 2
- dilations: int32 [2], replicated, may hold values from 1 to 64, as said below
- out_proj: bfloat16 [1024, 512], P('fsdp'), may hold values from -0.1875 to 0.1875
- cotangent: bfloat16 [4, 3072, 1024], P('fsdp', 'ctx'), may hold values from -0.0390625 to 0.0390625
Outputs:
- block_out: bfloat16 [4, 3072, 1024], P('fsdp', 'ctx')
- grad_in_proj: float32 [1024, 512], P('fsdp')
- grad_out_proj: float32 [1024, 512], P('fsdp')
- grad_taps: float32 [2, 7, 1024], replicated
Inputs may be any that keep to these rules, and one draw needn't show every extreme that they name: `dilations`: each dilation is a power of two; exactly one equals 64, the other is smaller.
All inputs are finite; a program needn't handle non-finite values.
Results may differ from a plain program's by a relative error of at most 0.0095.
Values may be sent and summed in bfloat16 or wider, within the bound.
A program may use at most 128 MiB of HBM per device.

v0:
```python
import functools

import jax
import jax.numpy as jnp
from jax import lax
from jax.experimental import pallas as pl
from jax.experimental.pallas import tpu as pltpu
from jax.sharding import PartitionSpec as P

KERNEL = 7
MAXDIL = 64
MARGIN = (KERNEL - 1) * MAXDIL
BLOCK = 128
CHUNK = 128
norm_eps = 1e-05
F32 = jnp.float32
BF16 = jnp.bfloat16


def passed_along(value, axis, by):
    length = lax.axis_size(axis)
    pairs = [(i, i + by) for i in range(length) if 0 <= i + by < length]
    return lax.ppermute(value, axis, pairs)


def normalize(strand, norm_gain):
    floats = strand.astype(F32)
    inverse = lax.rsqrt(jnp.mean(floats * floats, axis=-1, keepdims=True) + norm_eps)
    return (floats * inverse * norm_gain).astype(BF16)


def mm(a, b, dims):
    return lax.dot_general(a, b, (dims, ((), ())), preferred_element_type=F32)


def starts(d, ahead):
    return [d * (KERNEL - 1 - t) if ahead else MARGIN - d * (KERNEL - 1 - t) for t in range(KERNEL)]


def join(ext, s, value, rim, ahead):
    rows = value.shape[0]
    if ahead:
        ext[s, 0:rows] = value.astype(F32)
        ext[s, rows : rows + MARGIN] = rim.astype(F32)
    else:
        ext[s, 0:MARGIN] = rim.astype(F32)
        ext[s, MARGIN : MARGIN + rows] = value.astype(F32)


def conv(ext, s, w_ref, f, first, offsets):
    acc = None
    for t in range(KERNEL):
        term = w_ref[f, t : t + 1, :] * ext[s, pl.ds(first + offsets[t], CHUNK), :]
        acc = term if acc is None else acc + term
    return acc


def tap_terms(sums, grad, ext, s, first, offsets):
    out = []
    for t in range(KERNEL):
        prod = grad * ext[s, pl.ds(first + offsets[t], CHUNK), :]
        part = prod[0:8]
        for k in range(1, CHUNK // 8):
            part = part + prod[8 * k : 8 * k + 8]
        out.append(sums[t] + part)
    return out


def no_sums():
    return [jnp.zeros((8, BLOCK), F32) for _ in range(KERNEL)]


def put_sums(out_ref, sums):
    for t in range(KERNEL):
        out_ref[t : t + 1, :] = jnp.sum(sums[t], axis=0, keepdims=True)


def first_kernel(d_ref, w_ref, n_ref, p_ref, e_ref, o_ref, ext):
    rows = o_ref.shape[1]
    for s in range(2):
        e = mm(n_ref[s], p_ref[...], ((1,), (1,))).astype(BF16)
        e_ref[s] = e
        ext[s] = e.astype(F32)
    for s in range(2):
        offsets = starts(d_ref[0], s == 1)

        @pl.loop(0, rows // CHUNK)
        def _(i):
            r = pl.multiple_of(i * CHUNK, CHUNK)
            o_ref[s, pl.ds(r, CHUNK), :] = conv(ext, s, w_ref, 0, r, offsets).astype(BF16)


def second_kernel(d_ref, w_ref, f_ref, rim_ref, e_ref, u_ref, p_ref, gated_ref, sg_ref, act_ref, tg_ref, ext, hg):
    rows = f_ref.shape[1]
    for s in range(2):
        join(ext, s, f_ref[s], rim_ref[s], s == 1)
        hg[s] = mm(u_ref[s], p_ref[...], ((1,), (1,)))
    sums = no_sums()
    for s in range(2):
        offsets = starts(d_ref[1], s == 1)
        own = 0 if s == 1 else MARGIN

        def step(i, sums):
            r = pl.multiple_of(i * CHUNK, CHUNK)
            here = pl.ds(r, CHUNK)
            v = conv(ext, s, w_ref, 1, r, offsets)
            sig = jax.nn.sigmoid(v)
            act = v * sig
            e = e_ref[s, pl.ds(pl.multiple_of(own + r, CHUNK), CHUNK), :].astype(F32)
            h = hg[s, here, :]
            gated_ref[s, here, :] = (act * e).astype(BF16)
            act_ref[s, here, :] = h * act
            grad = (h * e * sig * (1.0 + v * (1.0 - sig))).astype(BF16)
            sg_ref[s, here, :] = grad
            return tap_terms(sums, grad.astype(F32), ext, s, r, offsets)

        sums = lax.fori_loop(0, rows // CHUNK, step, sums)
    put_sums(tg_ref, sums)


def third_kernel(d_ref, w_ref, sg_ref, rim_ref, e_ref, fg_ref, tg_ref, ext, eext):
    rows = sg_ref.shape[1]
    for s in range(2):
        join(ext, s, sg_ref[s], rim_ref[s], s == 0)
        eext[s] = e_ref[s].astype(F32)
    sums = no_sums()
    for s in range(2):
        offsets = starts(d_ref[1], s == 0)
        behind = starts(d_ref[0], s == 1)

        def step(i, sums):
            r = pl.multiple_of(i * CHUNK, CHUNK)
            grad = conv(ext, s, w_ref, 1, r, offsets).astype(BF16)
            fg_ref[s, pl.ds(r, CHUNK), :] = grad
            return tap_terms(sums, grad.astype(F32), eext, s, r, behind)

        sums = lax.fori_loop(0, rows // CHUNK, step, sums)
    put_sums(tg_ref, sums)


def fourth_kernel(d_ref, w_ref, fg_ref, rim_ref, act_ref, eg_ref, ext):
    rows = fg_ref.shape[1]
    for s in range(2):
        join(ext, s, fg_ref[s], rim_ref[s], s == 0)
    for s in range(2):
        offsets = starts(d_ref[0], s == 0)

        @pl.loop(0, rows // CHUNK)
        def _(i):
            r = pl.multiple_of(i * CHUNK, CHUNK)
            here = pl.ds(r, CHUNK)
            eg_ref[s, here, :] = (act_ref[s, here, :] + conv(ext, s, w_ref, 0, r, offsets)).astype(BF16)


def hidden_block(rows):
    return pl.BlockSpec((2, rows, BLOCK), lambda j: (0, 0, j))


def call(kernel, inner, in_specs, outs, scratch, args, ops):
    specs = [pl.BlockSpec(memory_space=pltpu.SMEM), pl.BlockSpec((2, KERNEL, BLOCK), lambda j: (0, 0, j))]
    return pl.pallas_call(
        kernel,
        grid=(inner // BLOCK,),
        in_specs=specs + in_specs,
        out_specs=[o[1] for o in outs],
        out_shape=[o[0] for o in outs],
        scratch_shapes=[pltpu.VMEM(s, F32) for s in scratch],
        compiler_params=pltpu.CompilerParams(vmem_limit_bytes=32 << 20),
        cost_estimate=pl.CostEstimate(flops=ops, bytes_accessed=8 << 20, transcendentals=0),
    )(*args)


def rims(values, backward):
    got = []
    for s in range(2):
        if (s == 1) != backward:
            got.append(passed_along(values[s][:MARGIN], "ctx", -1))
        else:
            got.append(passed_along(values[s][-MARGIN:], "ctx", 1))
    return got


def body(states, norm_gain, in_proj, conv_taps, dilations, out_proj, cotangent):
    half = states.shape[2] // 2
    rows = states.shape[1]
    inner = conv_taps.shape[2]
    full_in, full_out = weights(in_proj, out_proj)
    flip = jnp.eye(half, dtype=BF16)[::-1]

    def flipped(a):
        return mm(a, flip, ((1,), (0,))).astype(BF16)

    strand = [states[0, :, :half], flipped(states[0, :, half:])]
    ups = jnp.stack([cotangent[0, :, :half], flipped(cotangent[0, :, half:])])
    rim = rims(strand, False)
    ext = jnp.stack([jnp.concatenate([rim[0], strand[0]]), jnp.concatenate([strand[1], rim[1]])])
    normed_ext = normalize(ext, norm_gain)

    wide = rows + MARGIN
    proj = pl.BlockSpec((BLOCK, half), lambda j: (j, 0))
    whole_rows = pl.BlockSpec((2, rows, half), lambda j: (0, 0, 0))

    def out(n, dtype=BF16):
        return (jax.ShapeDtypeStruct((2, n, inner), dtype), hidden_block(n))

    tap_out = (jax.ShapeDtypeStruct((KERNEL, inner), F32), pl.BlockSpec((KERNEL, BLOCK), lambda j: (0, j)))
    scr = (2, wide, BLOCK)
    expanded, first = call(
        first_kernel, inner,
        [pl.BlockSpec((2, wide, half), lambda j: (0, 0, 0)), proj],
        [out(wide), out(rows)], [scr],
        (dilations, conv_taps, normed_ext, full_in), 2 * 10**9,
    )
    first_rim = jnp.stack(rims(first, False))
    gated, second_grad, act_term, tg1 = call(
        second_kernel, inner,
        [hidden_block(rows), hidden_block(MARGIN), hidden_block(wide), whole_rows, proj],
        [out(rows), out(rows), out(rows, F32), tap_out], [scr, (2, rows, BLOCK)],
        (dilations, conv_taps, first, first_rim, expanded, ups, full_out), 2 * 10**9,
    )
    second_rim = jnp.stack(rims(second_grad, True))
    flat_gated = gated.reshape(2 * rows, inner)
    grad_out = mm(flat_gated, ups.reshape(2 * rows, half), ((0,), (0,)))
    first_grad, tg0 = call(
        third_kernel, inner,
        [hidden_block(rows), hidden_block(MARGIN), hidden_block(wide)],
        [out(rows), tap_out], [scr, scr],
        (dilations, conv_taps, second_grad, second_rim, expanded), 10**9,
    )
    third_rim = jnp.stack(rims(first_grad, True))
    mixed = mm(flat_gated, full_out, ((1,), (0,))).reshape(2, rows, half)
    made = [(strand[s].astype(F32) + mixed[s]).astype(BF16) for s in range(2)]
    block_out = jnp.concatenate([made[0], flipped(made[1])], axis=1)[None]
    (exp_grad,) = call(
        fourth_kernel, inner,
        [hidden_block(rows), hidden_block(MARGIN), hidden_block(rows)],
        [out(rows)], [scr],
        (dilations, conv_taps, first_grad, third_rim, act_term), 10**9,
    )
    grad_in = sum(mm(exp_grad[s], normalize(strand[s], norm_gain), ((0,), (0,))) for s in range(2))
    return (block_out, *summed(grad_in, grad_out, jnp.stack([tg0, tg1])))


def weights(in_proj, out_proj):
    half = in_proj.shape[1]
    both = lax.all_gather(jnp.concatenate([in_proj, out_proj], axis=1), "fsdp", axis=0, tiled=True)
    return both[:, :half], both[:, half:]


def summed(grad_in, grad_out, taps):
    half = grad_in.shape[1]
    count = taps.shape[0] * taps.shape[1]
    cols = taps.reshape(count, taps.shape[2]).T
    packed = jnp.concatenate([grad_in, grad_out, jnp.pad(cols, ((0, 0), (0, 128 - count)))], axis=1).astype(BF16)
    packed = lax.psum(lax.psum_scatter(packed, "fsdp", scatter_dimension=0, tiled=True), "ctx")
    tap_rows = lax.all_gather(packed[:, 2 * half :], "fsdp", axis=0, tiled=True)
    grad_taps = tap_rows[:, :count].T.reshape(taps.shape)
    return packed[:, :half].astype(F32), packed[:, half : 2 * half].astype(F32), grad_taps.astype(F32)


def solution(mesh):
    return jax.shard_map(
        body,
        mesh=mesh,
        in_specs=(
            P("fsdp", "ctx", None),
            P(),
            P("fsdp", None),
            P(),
            P(),
            P("fsdp", None),
            P("fsdp", "ctx", None),
        ),
        out_specs=(P("fsdp", "ctx", None), P("fsdp", None), P("fsdp", None), P()),
        check_vma=False,
    )
```

profile of v0, /device:TPU:0, one launch (start us, length us, event | category | flops | bytes accessed | tf_op | source)
XLA Modules:
  0.0 297.8 jit_solution(10070998158400496030)
XLA Ops:
  7.2 0.0 all-gather.2.cloned.1.call-start
  7.2 1.9 pad_maximum_fusion.5
  9.2 0.0 all-gather.2.cloned.1.call-update
  9.2 0.0 reduce-scatter.2.cloned.1.call-start
  9.3 0.0 copy-start.10
  9.3 2.5 collective-permute-start
  11.9 0.6 rev.3
  12.5 0.5 fusion.11
  13.0 1.3 collective-permute-start.1
  14.3 0.1 maximum_bitcast_fusion
  14.4 0.0 copy-start.11
  14.4 4.3 %collective-permute-done.1 = bf16[384,512]{1,0:T(8,128)(2,1)S(1)} collective-permute-done((bf16[384,512]{1,0:T(8,128)(2,1)S(1)}, bf16[384,512]{1,0:T(8,128)(2,1)S(1)}, u32[]{:S(2)}, u32[]{:S(2)}) %collective-permute-start.1) | collective-permute-done | bytes 393248 | tf_op jit(solution)/shard_map/ppermute | solution.py:23
  18.6 0.1 maximum_bitcast_fusion.1
  18.7 0.4 fusion.1
  19.1 0.4 fusion.3.n_ref
  19.6 0.0 copy-start.2
  19.6 39.3 %all-gather.2.cloned.1.call-done = bf16[1024,1024]{1,0:T(8,128)(2,1)} async-done(((bf16[256,1024]{1,0:T(8,128)(2,1)}), bf16[1024,1024]{1,0:T(8,128)(2,1)}) %all-gather.2.cloned.1.call-update) | async-done | bytes 2097168 | tf_op jit(solution)/shard_map/all_gather | solution.py:246
  58.8 1.7 fusion.30
  60.5 8.3 %shard_map.102 = (bf16[2,768,1024]{2,1,0:T(8,128)(2,1)S(1)}, bf16[2,384,1024]{2,1,0:T(8,128)(2,1)S(1)}) custom-call(s32[2]{0:T(128)S(1)} %copy-done.2, f32[2,7,1024]{2,1,0:T(8,128)S(1)} %copy.26.w_ref, bf16[2,768,512]{2,1,0:T(8,128)(2,1)S(1)} %fusion.3.n_ref, bf16[1024,512]{1,0:T(8,128)(2,1)S(1)} %get-tuple-element.29.p_ref), custom_call_target="tpu_custom_call" | custom-call | flops 2000000000 | bytes 8388608 | tf_op jit(solution)/shard_map/pallas_call | solution.py:161
  68.9 0.0 copy-start.9
  68.9 0.1 slice_bitcast_fusion.9
  69.0 1.9 collective-permute-start.2
  70.9 1.3 collective-permute-start.3
  72.3 0.4 fusion.6
  72.6 0.1 pad_maximum_fusion.4.u_ref
  72.7 0.0 collective-permute-done.2
  72.8 3.6 %collective-permute-done.3 = bf16[384,1024]{1,0:T(8,128)(2,1)S(1)} collective-permute-done((bf16[384,1024]{1,0:T(8,128)(2,1)S(1)}, bf16[384,1024]{1,0:T(8,128)(2,1)S(1)}, u32[]{:S(2)}, u32[]{:S(2)}) %collective-permute-start.3) | collective-permute-done | bytes 786464 | tf_op jit(solution)/shard_map/ppermute | solution.py:23
  76.3 0.1 pad_maximum_fusion.1.rim_ref
  76.5 11.7 %shard_map.103 = (bf16[2,384,1024]{2,1,0:T(8,128)(2,1)S(1)}, bf16[2,384,1024]{2,1,0:T(8,128)(2,1)S(1)}, f32[2,384,1024]{2,1,0:T(8,128)S(1)}, f32[7,1024]{1,0:T(8,128)S(1)}) custom-call(s32[2]{0:T(128)S(1)} %copy-done.2, f32[2,7,1024]{2,1,0:T(8,128)S(1)} %copy.26.w_ref, bf16[2,384,1024]{2,1,0:T(8,128)(2,1)S(1)} %get-tuple-element.12.f_ref, ...), custom_call_target="tpu_custom_call" | custom-call | flops 2000000000 | bytes 8388608 | tf_op jit(solution)/shard_map/pallas_call | solution.py:161
  88.2 0.1 slice_bitcast_fusion.7
  88.3 1.5 copy-done
  89.8 1.4 collective-permute-start.4
  91.2 17.8 %collective-permute-start.5 = (bf16[384,1024]{1,0:T(8,128)(2,1)S(1)}, bf16[384,1024]{1,0:T(8,128)(2,1)S(1)}, u32[]{:S(2)}, u32[]{:S(2)}) collective-permute-start(bf16[384,1024]{1,0:T(8,128)(2,1)S(1)} %get-tuple-element.33), channel_id=1, source_target_pairs={{0,4},{4,8},{8,12},{12,16},{16,20},{20,24},{24,28},{1,5},{5,9},{9,... | collective-permute-start | bytes 2359304 | tf_op jit(solution)/shard_map/ppermute | solution.py:23
  109.1 1.0 fusion.28
  110.1 1.0 fusion.9
  111.1 0.0 collective-permute-done.4
  111.1 0.3 copy-done.5
  111.4 0.1 pad_maximum_fusion.2.rim_ref
  111.6 7.0 %shard_map.104 = (bf16[2,384,1024]{2,1,0:T(8,128)(2,1)S(1)}, f32[7,1024]{1,0:T(8,128)S(1)}) custom-call(s32[2]{0:T(128)S(1)} %copy-done.2, f32[2,7,1024]{2,1,0:T(8,128)S(1)} %copy.26.w_ref, bf16[2,384,1024]{2,1,0:T(8,128)(2,1)S(1)} %get-tuple-element.15.sg_ref, bf16[2,384,1024]{2,1,0:T(8,128)(2,1)S(1)} %pad_maximum_fusion.2.rim_ref, ...), custom_call_target="tpu_custom_call" | custom-call | flops 1000000000 | bytes 8388608 | tf_op jit(solution)/shard_map/pallas_call | solution.py:161
  118.6 1.3 slice_bitcast_fusion.5
  119.9 1.3 collective-permute-start.6
  121.1 15.2 %collective-permute-start.7 = (bf16[384,1024]{1,0:T(8,128)(2,1)}, bf16[384,1024]{1,0:T(8,128)(2,1)}, u32[]{:S(2)}, u32[]{:S(2)}) collective-permute-start(bf16[384,1024]{1,0:T(8,128)(2,1)} %get-tuple-element.31), channel_id=1, source_target_pairs={{0,4},{4,8},{8,12},{12,16},{16,20},{20,24},{24,28},{1,5},{5,9},{9,... | collective-permute-start | bytes 2359304 | tf_op jit(solution)/shard_map/ppermute | solution.py:23
  136.3 2.0 bitcast_convert_fusion
  138.4 1.7 pad_maximum_fusion.3.rim_ref
  140.1 0.7 copy-done.1
  140.8 4.6 %shard_map.105 = bf16[2,384,1024]{2,1,0:T(8,128)(2,1)S(1)} custom-call(s32[2]{0:T(128)S(1)} %copy-done.2, f32[2,7,1024]{2,1,0:T(8,128)S(1)} %copy.26.w_ref, bf16[2,384,1024]{2,1,0:T(8,128)(2,1)S(1)} %get-tuple-element.16.fg_ref, bf16[2,384,1024]{2,1,0:T(8,128)(2,1)S(1)} %pad_maximum_fusion.3.rim_ref, f32[2,384,1024]{2,1,0:T(8,128)S(1)} %copy-done.1), custom_call_target="tpu_custom_call" | custom-call | flops 1000000000 | bytes 8388608 | tf_op jit(solution)/shard_map/pallas_call | solution.py:161
  145.3 0.8 fusion.14
  146.2 0.8 add_convert_fusion
  147.0 0.4 copy-done.8
  147.4 1.6 fusion.4
  149.0 0.0 reduce-scatter.2.cloned.1.call-update
  149.1 0.0 copy-start.7
  149.1 0.0 all-reduce.3.cloned.1.call-start
  149.1 65.9 %reduce-scatter.2.cloned.1.call-done = bf16[256,1152]{0,1:T(8,128)(2,1)} async-done(((bf16[1024,1152]{0,1:T(8,128)(2,1)}), bf16[256,1152]{0,1:T(8,128)(2,1)}) %reduce-scatter.2.cloned.1.call-update) | async-done | bytes 589840 | tf_op jit(solution)/shard_map/reduce_scatter | solution.py:255
  215.0 0.0 all-reduce.3.cloned.1.call-update
  215.1 0.4 convolution_convert_fusion.2
  215.5 1.0 maximum_bitcast_fusion.2
  216.5 56.2 %all-reduce.3.cloned.1.call-done = bf16[256,1152]{0,1:T(8,128)(2,1)} async-done(((bf16[256,1152]{0,1:T(8,128)(2,1)}), bf16[256,1152]{0,1:T(8,128)(2,1)}) %all-reduce.3.cloned.1.call-update) | async-done | bytes 589840 | tf_op jit(solution)/shard_map/psum | solution.py:255
  272.7 0.8 slice.90
  273.5 13.9 %all_gather.7 = bf16[1024,128]{0,1:T(8,128)(2,1)S(1)} all-gather(bf16[256,128]{0,1:T(8,128)(2,1)S(1)} %slice.90), channel_id=1, replica_groups=mesh['ctx'=8,'fsdp'=4] {'fsdp'}, dimensions={0}, use_global_device_ids=true | all-gather | bytes 327680 | tf_op jit(solution)/shard_map/all_gather | solution.py:256
  287.5 0.7 copy.34
  288.1 1.1 slice_convert_fusion
  289.3 1.0 copy.33
  290.2 1.0 copy.32
  (32 shorter events, 0.2 us)
Async XLA Ops:
  7.2 2.1 copy-start.4
  7.2 51.6 %all-gather.2.cloned.1.call-start = ((), (), s32[]{:S(2)}) async-start(), calls=%async_computation.1 | async-start | bytes 2621440 | tf_op jit(solution)/shard_map/all_gather | solution.py:246
  9.2 205.9 %reduce-scatter.2.cloned.1.call-start = ((), (), s32[]{:S(2)}) async-start(), calls=%async_computation.2 | async-start | bytes 2949120 | tf_op jit(solution)/shard_map/reduce_scatter | solution.py:255
  9.3 5.0 %copy-start.10 = (f32[2,7,1024]{2,0,1:T(2,128)S(1)}, f32[2,7,1024]{2,0,1:T(2,128)}, u32[]{:S(2)}) copy-start(f32[2,7,1024]{2,0,1:T(2,128)} %param.10) | copy-start | bytes 172036
  9.3 5.0 %collective-permute-start = (bf16[384,512]{1,0:T(8,128)(2,1)S(1)}, bf16[384,512]{1,0:T(8,128)(2,1)S(1)}, u32[]{:S(2)}, u32[]{:S(2)}) collective-permute-start(bf16[384,512]{1,0:T(8,128)(2,1)S(1)} %slice_bitcast_fusion.10), channel_id=1, source_target_pairs={{0,4},{4,8},{8,12},{12,16},{16,20},{20,24},{24,28},{1,5},{5,9},{9,... | collective-permute-start | bytes 1179656 | tf_op jit(solution)/shard_map/ppermute | solution.py:23
  13.0 5.7 %collective-permute-start.1 = (bf16[384,512]{1,0:T(8,128)(2,1)S(1)}, bf16[384,512]{1,0:T(8,128)(2,1)S(1)}, u32[]{:S(2)}, u32[]{:S(2)}) collective-permute-start(bf16[384,512]{1,0:T(8,128)(2,1)S(1)} %get-tuple-element.41), channel_id=1, source_target_pairs={{4,0},{8,4},{12,8},{16,12},{20,16},{24,20},{28,24},{5,1},{9,5},{13... | collective-permute-start | bytes 1179656 | tf_op jit(solution)/shard_map/ppermute | solution.py:23
  14.4 4.7 %copy-start.11 = (f32[512]{0:T(512)S(1)}, f32[512]{0:T(512)}, u32[]{:S(2)}) copy-start(f32[512]{0:T(512)} %param.8) | copy-start | bytes 6148
  19.6 41.0 %copy-start.2 = (s32[2]{0:T(128)S(1)}, s32[2]{0:T(128)}, u32[]{:S(2)}) copy-start(s32[2]{0:T(128)} %d_ref.7) | copy-start | bytes 28
  68.9 3.4 %copy-start.9 = (bf16[1,384,1024]{2,1,0:T(8,128)(2,1)S(1)}, bf16[1,384,1024]{2,1,0:T(8,128)(2,1)}, u32[]{:S(2)}) copy-start(bf16[1,384,1024]{2,1,0:T(8,128)(2,1)} %param.13) | copy-start | bytes 2359300
  69.0 3.8 %collective-permute-start.2 = (bf16[384,1024]{1,0:T(8,128)(2,1)S(1)}, bf16[384,1024]{1,0:T(8,128)(2,1)S(1)}, u32[]{:S(2)}, u32[]{:S(2)}) collective-permute-start(bf16[384,1024]{1,0:T(8,128)(2,1)S(1)} %get-tuple-element.34), channel_id=1, source_target_pairs={{0,4},{4,8},{8,12},{12,16},{16,20},{20,24},{24,28},{1,5},{5,9},{9,... | collective-permute-start | bytes 2359304 | tf_op jit(solution)/shard_map/ppermute | solution.py:23
  70.9 5.4 %collective-permute-start.3 = (bf16[384,1024]{1,0:T(8,128)(2,1)S(1)}, bf16[384,1024]{1,0:T(8,128)(2,1)S(1)}, u32[]{:S(2)}, u32[]{:S(2)}) collective-permute-start(bf16[384,1024]{1,0:T(8,128)(2,1)S(1)} %get-tuple-element.35), channel_id=1, source_target_pairs={{4,0},{8,4},{12,8},{16,12},{20,16},{24,20},{28,24},{5,1},{9,5},{13... | collective-permute-start | bytes 2359304 | tf_op jit(solution)/shard_map/ppermute | solution.py:23
  88.2 1.6 copy-start
  88.2 20.9 %copy-start.3 = (bf16[1024,1024]{1,0:T(8,128)(2,1)S(1)}, bf16[1024,1024]{1,0:T(8,128)(2,1)}, u32[]{:S(2)}) copy-start(bf16[1024,1024]{1,0:T(8,128)(2,1)} %all-gather.2.cloned.1.call-done) | copy-start | bytes 6291460
  89.8 21.3 %collective-permute-start.4 = (bf16[384,1024]{1,0:T(8,128)(2,1)S(1)}, bf16[384,1024]{1,0:T(8,128)(2,1)S(1)}, u32[]{:S(2)}, u32[]{:S(2)}) collective-permute-start(bf16[384,1024]{1,0:T(8,128)(2,1)S(1)} %get-tuple-element.32), channel_id=1, source_target_pairs={{4,0},{8,4},{12,8},{16,12},{20,16},{24,20},{28,24},{5,1},{9,5},{13... | collective-permute-start | bytes 2359304 | tf_op jit(solution)/shard_map/ppermute | solution.py:23
  91.2 19.9 %collective-permute-start.5 = (bf16[384,1024]{1,0:T(8,128)(2,1)S(1)}, bf16[384,1024]{1,0:T(8,128)(2,1)S(1)}, u32[]{:S(2)}, u32[]{:S(2)}) collective-permute-start(bf16[384,1024]{1,0:T(8,128)(2,1)S(1)} %get-tuple-element.33), channel_id=1, source_target_pairs={{0,4},{4,8},{8,12},{12,16},{16,20},{20,24},{24,28},{1,5},{5,9},{9,... | collective-permute-start | bytes 2359304 | tf_op jit(solution)/shard_map/ppermute | solution.py:23
  110.1 1.3 copy-start.5
  119.9 18.5 %collective-permute-start.6 = (bf16[384,1024]{1,0:T(8,128)(2,1)}, bf16[384,1024]{1,0:T(8,128)(2,1)}, u32[]{:S(2)}, u32[]{:S(2)}) collective-permute-start(bf16[384,1024]{1,0:T(8,128)(2,1)} %get-tuple-element.30), channel_id=1, source_target_pairs={{4,0},{8,4},{12,8},{16,12},{20,16},{24,20},{28,24},{5,1},{9,5},{13... | collective-permute-start | bytes 2359304 | tf_op jit(solution)/shard_map/ppermute | solution.py:23
  121.1 17.2 %collective-permute-start.7 = (bf16[384,1024]{1,0:T(8,128)(2,1)}, bf16[384,1024]{1,0:T(8,128)(2,1)}, u32[]{:S(2)}, u32[]{:S(2)}) collective-permute-start(bf16[384,1024]{1,0:T(8,128)(2,1)} %get-tuple-element.31), channel_id=1, source_target_pairs={{0,4},{4,8},{8,12},{12,16},{16,20},{20,24},{24,28},{1,5},{5,9},{9,... | collective-permute-start | bytes 2359304 | tf_op jit(solution)/shard_map/ppermute | solution.py:23
  138.4 2.4 copy-start.1
  146.2 1.2 copy-start.8
  149.0 66.0 %copy-start.6 = (f32[768,512]{1,0:T(8,128)S(1)}, f32[768,512]{1,0:T(8,128)}, u32[]{:S(2)}) copy-start(f32[768,512]{1,0:T(8,128)} %copy-done.5) | copy-start | bytes 4718596
  149.1 66.4 %copy-start.7 = (bf16[384,512]{1,0:T(8,128)(2,1)S(1)}, bf16[384,512]{1,0:T(8,128)(2,1)}, u32[]{:S(2)}) copy-start(bf16[384,512]{1,0:T(8,128)(2,1)} %get-tuple-element.37) | copy-start | bytes 1179652
  149.1 123.6 %all-reduce.3.cloned.1.call-start = ((), (), s32[]{:S(2)}) async-start(), calls=%async_computation.3 | async-start | bytes 1179648 | tf_op jit(solution)/shard_map/psum | solution.py:255
Sparse Core Ops, SparseCore 0:
  10.2 48.6 all-gather.1
  149.2 65.8 reduce-scatter.1
  218.2 54.4 all-reduce.2
where the time goes:
time: 298 us
  waiting for transfers between devices  169 us (57%)
  starting transfers between devices  42.8 us (14%)
  Pallas kernels  31.6 us (11%)
  between operations  14.2 us (5%)
  blocking collectives  13.9 us (5%)
  local copies, waits for them, and re-layouts  10.3 us (3%)
  other arithmetic  9.69 us (3%)
  matrix products  5.87 us (2%)
    reduce_scatter x1, waiting for transfers between devices, summed(): lax.psum_scatter(packed, 'fsdp', scatter_dimension=0, tiled=True)  65.9 us
    psum x1, waiting for transfers between devices, summed(): lax.psum(lax.psum_scatter(packed, 'fsdp', scatter_dimension=0, tiled=True...  56.2 us
    ppermute x8, starting transfers between devices, passed_along(): return lax.ppermute(value, axis, pairs)  42.7 us
    all_gather x1, waiting for transfers between devices, weights(): lax.all_gather(jnp.concatenate([in_proj, out_proj], axis=1), 'fsdp', axis...  39.3 us
    pallas_call x4, Pallas kernels, call(): pl.pallas_call(kernel, grid=(inner // BLOCK,), in_specs=specs + in_specs,...  31.6 us
    all_gather x1, blocking collectives, summed(): tap_rows = lax.all_gather(packed[:, 2 * half:], 'fsdp', axis=0, tiled=True)  13.9 us
    ppermute x8, waiting for transfers between devices, passed_along(): return lax.ppermute(value, axis, pairs)  7.87 us
  transfers between devices with their start and end apart: 11, of which 5 were waited for; matrix products, arithmetic and copies ran while one was open for 3% of the time, Pallas kernels for 0%

commit v1 on v0

--- a/solution.py
+++ b/solution.py
@@ -241,21 +241,61 @@
     return (block_out, *summed(grad_in, grad_out, jnp.stack([tg0, tg1])))
 
 
+def gathered(x, axis):
+    n = lax.axis_size(axis)
+    me = lax.axis_index(axis)
+    parts = lax.dynamic_update_slice_in_dim(jnp.zeros((n, *x.shape), x.dtype), x[None], me, 0)
+    for k in range(1, n):
+        got = lax.ppermute(x, axis, [(i, (i + k) % n) for i in range(n)])
+        parts = lax.dynamic_update_slice_in_dim(parts, got[None], (me - k + n) % n, 0)
+    return parts.reshape(n * x.shape[0], *x.shape[1:])
+
+
+def swapped(x, bit):
+    return lax.ppermute(x, "ctx", [(i, i ^ (1 << bit)) for i in range(lax.axis_size("ctx"))])
+
+
 def weights(in_proj, out_proj):
-    half = in_proj.shape[1]
-    both = lax.all_gather(jnp.concatenate([in_proj, out_proj], axis=1), "fsdp", axis=0, tiled=True)
-    return both[:, :half], both[:, half:]
+    even = lax.axis_index("ctx") % 2 == 0
+    mine = gathered(jnp.where(even, in_proj, out_proj), "fsdp")
+    other = swapped(mine, 0)
+    return jnp.where(even, mine, other), jnp.where(even, other, mine)
 
 
 def summed(grad_in, grad_out, taps):
     half = grad_in.shape[1]
     count = taps.shape[0] * taps.shape[1]
+    owners = lax.axis_size("fsdp")
+    per = grad_in.shape[0] // owners
+    me = lax.axis_index("ctx")
+    zone = lax.axis_index("fsdp")
+    bits = lax.axis_size("ctx").bit_length() - 1
     cols = taps.reshape(count, taps.shape[2]).T
-    packed = jnp.concatenate([grad_in, grad_out, jnp.pad(cols, ((0, 0), (0, 128 - count)))], axis=1).astype(BF16)
-    packed = lax.psum(lax.psum_scatter(packed, "fsdp", scatter_dimension=0, tiled=True), "ctx")
-    tap_rows = lax.all_gather(packed[:, 2 * half :], "fsdp", axis=0, tiled=True)
+    packed = jnp.concatenate([grad_in, grad_out, jnp.pad(cols, ((0, 0), (0, 128 - count)))], axis=1)
+    groups = packed.shape[1] // 128
+    x = packed.reshape(owners, per, groups, 128).transpose(0, 2, 1, 3).reshape(owners, groups * per, 128)
+    for bit in range(bits):
+        upper = (me >> bit) % 2 == 1
+        middle = x.shape[1] // 2
+        low, high = x[:, :middle], x[:, middle:]
+        got = swapped(jnp.where(upper, low, high).astype(BF16), bit)
+        x = jnp.where(upper, high, low) + got.astype(F32)
+    total = lax.dynamic_index_in_dim(x, zone, 0, False)
+    sent = x.astype(BF16)
+    for k in range(1, owners):
+        piece = lax.dynamic_index_in_dim(sent, (zone + k) % owners, 0, False)
+        got = lax.ppermute(piece, "fsdp", [(i, (i + k) % owners) for i in range(owners)])
+        total = total + got.astype(F32)
+    x = total.astype(BF16)
+    for bit in reversed(range(bits)):
+        upper = (me >> bit) % 2 == 1
+        got = swapped(x, bit)
+        x = jnp.concatenate([jnp.where(upper, got, x), jnp.where(upper, x, got)], axis=0)
+    x = x.reshape(groups, per, 128)
+    wide = x[:-1].transpose(1, 0, 2).reshape(per, 2 * half)
+    tap_rows = gathered(x[-1], "fsdp")
     grad_taps = tap_rows[:, :count].T.reshape(taps.shape)
-    return packed[:, :half].astype(F32), packed[:, half : 2 * half].astype(F32), grad_taps.astype(F32)
+    return wide[:, :half].astype(F32), wide[:, half:].astype(F32), grad_taps.astype(F32)
 
 
 def solution(mesh):

time: 298 us -> 229 us (0.77)
  waiting for transfers between devices: 169 us -> 50 us
  starting transfers between devices: 42.8 us -> 86.4 us
  local copies, waits for them, and re-layouts: 10.3 us -> 30.4 us
  blocking collectives: 13.9 us -> 0 us
  between operations: 14.2 us -> 1.46 us
  other arithmetic: 9.69 us -> 18.9 us
    reduce_scatter x1 -> x0, waiting for transfers between devices: 65.9 us -> none  [summed(): lax.psum_scatter(packed, 'fsdp', scatter_dimension=0, tiled=True)]
    psum x1 -> x0, waiting for transfers between devices: 56.2 us -> none  [summed(): lax.psum(lax.psum_scatter(packed, 'fsdp', scatter_dimension=0, tiled=True...]
    ppermute x0 -> x16, waiting for transfers between devices: none -> 47.1 us  [the longest x7 30.1 us: swapped(): lax.ppermute(x, 'ctx', [(i, i ^ 1 << bit) for i in range(lax.axis_size('c...]
    ppermute x0 -> x16, starting transfers between devices: none -> 43 us  [the longest x7 24.3 us: swapped(): lax.ppermute(x, 'ctx', [(i, i ^ 1 << bit) for i in range(lax.axis_size('c...]
    all_gather x1 -> x0, waiting for transfers between devices: 39.3 us -> none  [weights(): lax.all_gather(jnp.concatenate([in_proj, out_proj], axis=1), 'fsdp', axis...]
    all_gather x1 -> x0, blocking collectives: 13.9 us -> none  [summed(): tap_rows = lax.all_gather(packed[:, 2 * half:], 'fsdp', axis=0, tiled=True)]
    reshape x0 -> x2, local copies, waits for them, and re-layouts: none -> 13.1 us  [summed(): packed.reshape(owners, per, groups, 128).transpose(0, 2, 1, 3)]
    ppermute x8, waiting for transfers between devices: 7.87 us -> 2.94 us  [passed_along(): return lax.ppermute(value, axis, pairs)]
  transfers between devices with their start and end apart: 11 -> 24, of which waited for: 5 -> 13; matrix products, arithmetic and copies ran while one was open for 3% -> 8% of each run, Pallas kernels for 0% -> 0%
where the time goes in v1:
time: 229 us; the launch traced here: 228 us
  starting transfers between devices  86.4 us (38%)
  waiting for transfers between devices  50 us (22%)
  Pallas kernels  33.1 us (14%)
  local copies, waits for them, and re-layouts  30.4 us (13%)
  other arithmetic  18.9 us (8%)
  matrix products  7.9 us (3%)
    ppermute x8, starting transfers between devices, passed_along(): return lax.ppermute(value, axis, pairs)  43.4 us
    pallas_call x4, Pallas kernels, call(): pl.pallas_call(kernel, grid=(inner // BLOCK,), in_specs=specs + in_specs,...  33.1 us
    ppermute x7, waiting for transfers between devices, swapped(): lax.ppermute(x, 'ctx', [(i, i ^ 1 << bit) for i in range(lax.axis_size('c...  30.1 us
    ppermute x7, starting transfers between devices, swapped(): lax.ppermute(x, 'ctx', [(i, i ^ 1 << bit) for i in range(lax.axis_size('c...  24.3 us
    reshape x2, local copies, waits for them, and re-layouts, summed(): packed.reshape(owners, per, groups, 128).transpose(0, 2, 1, 3)  13.1 us
    ppermute x6, waiting for transfers between devices, gathered(): got = lax.ppermute(x, axis, [(i, (i + k) % n) for i in range(n)])  12.1 us
    ppermute x6, starting transfers between devices, gathered(): got = lax.ppermute(x, axis, [(i, (i + k) % n) for i in range(n)])  10.9 us
    unnamed x61, local copies, waits for them, and re-layouts  8.35 us
  transfers between devices with their start and end apart: 24, of which 13 were waited for; matrix products, arithmetic and copies ran while one was open for 8% of the time, Pallas kernels for 0%

profile of v1, /device:TPU:0, one launch (start us, length us, event | category | flops | bytes accessed | tf_op | source)
XLA Modules:
  0.0 228.1 jit_solution(7380267626659228669)
XLA Ops:
  0.7 1.1 bitcast_dynamic-update-slice_fusion.3
  1.8 3.1 %collective-permute-start.2 = (bf16[256,512]{1,0:T(8,128)(2,1)S(1)}, bf16[256,512]{1,0:T(8,128)(2,1)}, u32[]{:S(2)}, u32[]{:S(2)}) collective-permute-start(bf16[256,512]{1,0:T(8,128)(2,1)S(1)} %get-tuple-element.31), channel_id=1, source_target_pairs={{0,1},{1,2},{2,3},{3,0},{4,5},{5,6},{6,7},{7,4},{8,9},{9,10},{10,1... | collective-permute-start | bytes 786440 | tf_op jit(solution)/shard_map/ppermute | solution.py:249
  4.9 2.6 %collective-permute-start.3 = (bf16[256,512]{1,0:T(8,128)(2,1)S(1)}, bf16[256,512]{1,0:T(8,128)(2,1)}, u32[]{:S(2)}, u32[]{:S(2)}) collective-permute-start(bf16[256,512]{1,0:T(8,128)(2,1)S(1)} %get-tuple-element.31), channel_id=1, source_target_pairs={{0,2},{1,3},{2,0},{3,1},{4,6},{5,7},{6,4},{7,5},{8,10},{9,11},{10,... | collective-permute-start | bytes 786440 | tf_op jit(solution)/shard_map/ppermute | solution.py:249
  7.5 1.3 collective-permute-start.4
  8.9 0.6 rev.3
  10.0 1.3 collective-permute-start.1
  11.4 3.1 %collective-permute-start = (bf16[384,512]{1,0:T(8,128)(2,1)S(1)}, bf16[384,512]{1,0:T(8,128)(2,1)S(1)}, u32[]{:S(2)}, u32[]{:S(2)}) collective-permute-start(bf16[384,512]{1,0:T(8,128)(2,1)S(1)} %slice_bitcast_fusion.10), channel_id=1, source_target_pairs={{0,4},{4,8},{8,12},{12,16},{16,20},{20,24},{24,28},{1,5},{5,9},{9,... | collective-permute-start | bytes 1179656 | tf_op jit(solution)/shard_map/ppermute | solution.py:23
  14.5 1.0 bitcast_dynamic-update-slice_fusion.2
  15.5 9.3 %collective-permute-done.3 = bf16[256,512]{1,0:T(8,128)(2,1)} collective-permute-done((bf16[256,512]{1,0:T(8,128)(2,1)S(1)}, bf16[256,512]{1,0:T(8,128)(2,1)}, u32[]{:S(2)}, u32[]{:S(2)}) %collective-permute-start.3) | collective-permute-done | bytes 262176 | tf_op jit(solution)/shard_map/ppermute | solution.py:249
  24.7 1.0 bitcast_dynamic-update-slice_fusion.1
  25.7 1.0 bitcast_dynamic-update-slice_fusion
  26.8 0.8 copy.36.w_ref
  27.6 1.0 maximum_bitcast_fusion.1
  30.5 8.3 %shard_map.102 = (bf16[2,768,1024]{2,1,0:T(8,128)(2,1)S(1)}, bf16[2,384,1024]{2,1,0:T(8,128)(2,1)S(1)}) custom-call(s32[2]{0:T(128)S(1)} %copy-done.7, f32[2,7,1024]{2,1,0:T(8,128)S(1)} %copy.36.w_ref, bf16[2,768,512]{2,1,0:T(8,128)(2,1)S(1)} %fusion.2.n_ref, bf16[1024,512]{1,0:T(8,128)(2,1)S(1)} %get-tuple-element.33.p_ref), custom_call_target="tpu_custom_call" | custom-call | flops 2000000000 | bytes 8388608 | tf_op jit(solution)/shard_map/pallas_call | solution.py:161
  38.9 2.6 %collective-permute-start.6 = (bf16[384,1024]{1,0:T(8,128)(2,1)S(1)}, bf16[384,1024]{1,0:T(8,128)(2,1)S(1)}, u32[]{:S(2)}, u32[]{:S(2)}) collective-permute-start(bf16[384,1024]{1,0:T(8,128)(2,1)S(1)} %get-tuple-element.38), channel_id=1, source_target_pairs={{0,4},{4,8},{8,12},{12,16},{16,20},{20,24},{24,28},{1,5},{5,9},{9,... | collective-permute-start | bytes 2359304 | tf_op jit(solution)/shard_map/ppermute | solution.py:23
  41.5 1.3 collective-permute-start.7
  43.4 2.9 %collective-permute-done.7 = bf16[384,1024]{1,0:T(8,128)(2,1)S(1)} collective-permute-done((bf16[384,1024]{1,0:T(8,128)(2,1)S(1)}, bf16[384,1024]{1,0:T(8,128)(2,1)S(1)}, u32[]{:S(2)}, u32[]{:S(2)}) %collective-permute-start.7) | collective-permute-done | bytes 786464 | tf_op jit(solution)/shard_map/ppermute | solution.py:23
  46.4 12.6 %shard_map.103 = (bf16[2,384,1024]{2,1,0:T(8,128)(2,1)S(1)}, bf16[2,384,1024]{2,1,0:T(8,128)(2,1)S(1)}, f32[2,384,1024]{2,1,0:T(8,128)S(1)}, f32[7,1024]{1,0:T(8,128)S(1)}) custom-call(s32[2]{0:T(128)S(1)} %copy-done.7, f32[2,7,1024]{2,1,0:T(8,128)S(1)} %copy.36.w_ref, bf16[2,384,1024]{2,1,0:T(8,128)(2,1)S(1)} %get-tuple-element.12.f_ref, ...), custom_call_target="tpu_custom_call" | custom-call | flops 2000000000 | bytes 8388608 | tf_op jit(solution)/shard_map/pallas_call | solution.py:161
  59.1 1.6 copy-done.5
  60.7 1.5 slice_bitcast_fusion.7
  62.9 1.3 collective-permute-start.8
  64.2 18.8 %collective-permute-start.9 = (bf16[384,1024]{1,0:T(8,128)(2,1)}, bf16[384,1024]{1,0:T(8,128)(2,1)}, u32[]{:S(2)}, u32[]{:S(2)}) collective-permute-start(bf16[384,1024]{1,0:T(8,128)(2,1)} %get-tuple-element.37), channel_id=1, source_target_pairs={{0,4},{4,8},{8,12},{12,16},{16,20},{20,24},{24,28},{1,5},{5,9},{9,... | collective-permute-start | bytes 2359304 | tf_op jit(solution)/shard_map/ppermute | solution.py:23
  83.0 2.7 %fusion.30 = f32[768,512]{1,0:T(8,128)S(1)} fusion(bf16[768,1024]{1,0:T(8,128)(2,1)} %bitcast.114, bf16[1024,512]{1,0:T(8,128)(2,1)} %copy-done.4), kind=kOutput, calls=%fused_computation.96 | convolution fusion | flops 805306368 | bytes 4194304 | tf_op jit(solution)/shard_map/dot_general | solution.py:33
  85.7 2.1 pad_maximum_fusion.2.rim_ref
  88.1 7.6 %shard_map.104 = (bf16[2,384,1024]{2,1,0:T(8,128)(2,1)S(1)}, f32[7,1024]{1,0:T(8,128)S(1)}) custom-call(s32[2]{0:T(128)S(1)} %copy-done.7, f32[2,7,1024]{2,1,0:T(8,128)S(1)} %copy.36.w_ref, bf16[2,384,1024]{2,1,0:T(8,128)(2,1)S(1)} %copy-done.1, bf16[2,384,1024]{2,1,0:T(8,128)(2,1)S(1)} %pad_maximum_fusion.2.rim_ref, ...), custom_call_target="tpu_custom_call" | custom-call | flops 1000000000 | bytes 8388608 | tf_op jit(solution)/shard_map/pallas_call | solution.py:161
  95.7 1.3 slice_bitcast_fusion.5
  97.4 1.4 collective-permute-start.10
  98.8 13.7 %collective-permute-start.11 = (bf16[384,1024]{1,0:T(8,128)(2,1)}, bf16[384,1024]{1,0:T(8,128)(2,1)}, u32[]{:S(2)}, u32[]{:S(2)}) collective-permute-start(bf16[384,1024]{1,0:T(8,128)(2,1)} %get-tuple-element.35), channel_id=1, source_target_pairs={{0,4},{4,8},{8,12},{12,16},{16,20},{20,24},{24,28},{1,5},{5,9},{9,... | collective-permute-start | bytes 2359304 | tf_op jit(solution)/shard_map/ppermute | solution.py:23
  112.5 0.9 fusion.7
  113.4 2.4 %convolution_bitcast_fusion = f32[1024,512]{0,1:T(8,128)} fusion(bf16[2,384,1024]{2,1,0:T(8,128)(2,1)S(1)} %copy-done.9, bf16[1,384,512]{2,1,0:T(8,128)(2,1)S(1)} %copy-done.25, bf16[1,384,512]{2,1,0:T(8,128)(2,1)S(1)} %copy-done.22), kind=kOutput, calls=%fused_computation.10 | convolution fusion | flops 805699584 | bytes 4456448 | tf_op jit(solution)/shard_map/dot_general | solution.py:33
  115.8 1.6 pad_maximum_fusion.3.rim_ref
  117.7 4.6 %shard_map.105 = bf16[2,384,1024]{2,1,0:T(8,128)(2,1)S(1)} custom-call(s32[2]{0:T(128)S(1)} %copy-done.7, f32[2,7,1024]{2,1,0:T(8,128)S(1)} %copy.36.w_ref, bf16[2,384,1024]{2,1,0:T(8,128)(2,1)S(1)} %copy-done.3, bf16[2,384,1024]{2,1,0:T(8,128)(2,1)S(1)} %pad_maximum_fusion.3.rim_ref, f32[2,384,1024]{2,1,0:T(8,128)S(1)} %copy-done.6), custom_call_target="tpu_custom_call" | custom-call | flops 1000000000 | bytes 8388608 | tf_op jit(solution)/shard_map/pallas_call | solution.py:161
  122.3 0.8 fusion.12
  123.3 0.8 convolution_add_fusion
  124.1 0.7 copy-done.15
  124.9 2.6 %select_maximum_fusion = f32[1024,1152]{0,1:T(8,128)} fusion(f32[1024,14]{0,1:T(8,128)S(1)} %bitcast.124, f32[1024,512]{0,1:T(8,128)S(1)} %copy-done.15, f32[1024,512]{0,1:T(8,128)S(1)} %convolution_add_fusion), kind=kLoop, calls=%fused_computation | loop fusion | flops 4718592 | bytes 8970240 | tf_op jit(solution)/shard_map/concatenate | solution.py:274
  127.4 6.7 %reshape.85 = f32[4,256,9,128]{1,0,3,2:T(4,128)} reshape(f32[1024,1152]{0,1:T(8,128)} %select_maximum_fusion) | data formatting | bytes 9437184 | tf_op jit(solution)/shard_map/reshape | solution.py:276
  134.1 6.5 %copy.42 = f32[4,256,9,128]{3,1,2,0:T(8,128)} copy(f32[4,256,9,128]{1,0,3,2:T(4,128)} %reshape.85) | data formatting | bytes 9437184 | tf_op jit(solution)/shard_map/reshape | solution.py:276
  140.6 2.6 %select_convert_fusion = bf16[4,1152,128]{2,1,0:T(8,128)(2,1)S(1)} fusion(f32[4,2304,128]{2,1,0:T(8,128)} %bitcast.115, pred[]{:T(512)S(6)} %eq.37), kind=kLoop, calls=%fused_computation.8 | loop fusion | flops 589824 | bytes 3538945 | tf_op jit(solution)/shard_map/convert_element_type | solution.py:281
  143.1 6.8 %collective-permute-start.12 = (bf16[4,1152,128]{2,1,0:T(8,128)(2,1)S(1)}, bf16[4,1152,128]{2,1,0:T(8,128)(2,1)}, u32[]{:S(2)}, u32[]{:S(2)}) collective-permute-start(bf16[4,1152,128]{2,1,0:T(8,128)(2,1)S(1)} %select_convert_fusion), channel_id=1, source_target_pairs={{0,4},{4,0},{8,12},{12,8},{16,20},{20,16},{24,28},{28,24},{1,5},{5... | collective-permute-start | bytes 3538952 | tf_op jit(solution)/shard_map/ppermute | solution.py:255
  149.9 2.6 %collective-permute-done.12 = bf16[4,1152,128]{2,1,0:T(8,128)(2,1)} collective-permute-done((bf16[4,1152,128]{2,1,0:T(8,128)(2,1)S(1)}, bf16[4,1152,128]{2,1,0:T(8,128)(2,1)}, u32[]{:S(2)}, u32[]{:S(2)}) %collective-permute-start.12) | collective-permute-done | bytes 1179680 | tf_op jit(solution)/shard_map/ppermute | solution.py:255
  152.5 3.0 %convert_add_fusion = f32[4,1152,128]{2,1,0:T(8,128)S(1)} fusion(bf16[4,1152,128]{2,1,0:T(8,128)(2,1)} %collective-permute-done.12, f32[4,2304,128]{2,1,0:T(8,128)} %bitcast.116, pred[]{:T(512)S(6)} %eq.37), kind=kLoop, calls=%fused_computation.7 | loop fusion | flops 1769472 | bytes 8257537 | tf_op jit(solution)/shard_map/add | solution.py:282
  155.5 0.9 select_convert_fusion.1
  156.5 12.3 %collective-permute-start.13 = (bf16[4,576,128]{2,1,0:T(8,128)(2,1)}, bf16[4,576,128]{2,1,0:T(8,128)(2,1)S(1)}, u32[]{:S(2)}, u32[]{:S(2)}) collective-permute-start(bf16[4,576,128]{2,1,0:T(8,128)(2,1)} %select_convert_fusion.1), channel_id=1, source_target_pairs={{0,8},{4,12},{8,0},{12,4},{16,24},{20,28},{24,16},{28,20},{1,9},{5... | collective-permute-start | bytes 1769480 | tf_op jit(solution)/shard_map/ppermute | solution.py:255
  168.8 14.1 %collective-permute-done.13 = bf16[4,576,128]{2,1,0:T(8,128)(2,1)S(1)} collective-permute-done((bf16[4,576,128]{2,1,0:T(8,128)(2,1)}, bf16[4,576,128]{2,1,0:T(8,128)(2,1)S(1)}, u32[]{:S(2)}, u32[]{:S(2)}) %collective-permute-start.13) | collective-permute-done | bytes 589856 | tf_op jit(solution)/shard_map/ppermute | solution.py:255
  183.0 1.9 collective-permute-start.14
  185.0 6.8 %collective-permute-done.14 = bf16[4,288,128]{2,1,0:T(8,128)(2,1)S(1)} collective-permute-done((bf16[4,288,128]{2,1,0:T(8,128)(2,1)S(1)}, bf16[4,288,128]{2,1,0:T(8,128)(2,1)S(1)}, u32[]{:S(2)}, u32[]{:S(2)}) %collective-permute-start.14) | collective-permute-done | bytes 294944 | tf_op jit(solution)/shard_map/ppermute | solution.py:255
  192.0 5.2 %collective-permute-start.15 = (bf16[288,128]{1,0:T(8,128)(2,1)S(1)}, bf16[288,128]{1,0:T(8,128)(2,1)S(1)}, u32[]{:S(2)}, u32[]{:S(2)}) collective-permute-start(bf16[288,128]{1,0:T(8,128)(2,1)S(1)} %get-tuple-element.48), channel_id=1, source_target_pairs={{0,1},{1,2},{2,3},{3,0},{4,5},{5,6},{6,7},{7,4},{8,9},{9,10},{10,1... | collective-permute-start | bytes 221192 | tf_op jit(solution)/shard_map/ppermute | solution.py:287
  197.2 2.6 %collective-permute-start.16 = (bf16[288,128]{1,0:T(8,128)(2,1)S(1)}, bf16[288,128]{1,0:T(8,128)(2,1)S(1)}, u32[]{:S(2)}, u32[]{:S(2)}) collective-permute-start(bf16[288,128]{1,0:T(8,128)(2,1)S(1)} %get-tuple-element.50), channel_id=1, source_target_pairs={{0,2},{1,3},{2,0},{3,1},{4,6},{5,7},{6,4},{7,5},{8,10},{9,11},{10,... | collective-permute-start | bytes 221192 | tf_op jit(solution)/shard_map/ppermute | solution.py:287
  199.7 2.5 %collective-permute-done.15 = bf16[288,128]{1,0:T(8,128)(2,1)S(1)} collective-permute-done((bf16[288,128]{1,0:T(8,128)(2,1)S(1)}, bf16[288,128]{1,0:T(8,128)(2,1)S(1)}, u32[]{:S(2)}, u32[]{:S(2)}) %collective-permute-start.15) | collective-permute-done | bytes 73760 | tf_op jit(solution)/shard_map/ppermute | solution.py:287
  202.2 2.2 collective-permute-done.16
  204.7 1.7 collective-permute-start.18
  206.4 2.7 %collective-permute-done.18 = bf16[288,128]{1,0:T(8,128)(2,1)S(1)} collective-permute-done((bf16[288,128]{1,0:T(8,128)(2,1)S(1)}, bf16[288,128]{1,0:T(8,128)(2,1)S(1)}, u32[]{:S(2)}, u32[]{:S(2)}) %collective-permute-start.18) | collective-permute-done | bytes 73760 | tf_op jit(solution)/shard_map/ppermute | solution.py:255
  209.2 1.5 collective-permute-start.19
  210.7 3.7 %collective-permute-done.19 = bf16[576,128]{1,0:T(8,128)(2,1)S(1)} collective-permute-done((bf16[576,128]{1,0:T(8,128)(2,1)S(1)}, bf16[576,128]{1,0:T(8,128)(2,1)S(1)}, u32[]{:S(2)}, u32[]{:S(2)}) %collective-permute-start.19) | collective-permute-done | bytes 147488 | tf_op jit(solution)/shard_map/ppermute | solution.py:255
  215.0 1.0 maximum_bitcast_fusion.2
  216.3 1.2 collective-permute-start.21
  217.5 1.9 collective-permute-start.22
  219.4 0.7 collective-permute-start.23
  220.5 1.0 copy.46
  221.5 1.0 copy.47
  223.1 2.2 collective-permute-done.22
  225.7 1.7 dynamic_update_slice.31
  227.5 0.7 copy.48
  (113 shorter events, 7.8 us)
Async XLA Ops:
  0.7 8.8 %copy-start.16 = (bf16[1,384,1024]{2,1,0:T(8,128)(2,1)S(1)}, bf16[1,384,1024]{2,1,0:T(8,128)(2,1)}, u32[]{:S(2)}) copy-start(bf16[1,384,1024]{2,1,0:T(8,128)(2,1)} %param.7) | copy-start | bytes 2359300
  1.8 12.6 %collective-permute-start.2 = (bf16[256,512]{1,0:T(8,128)(2,1)S(1)}, bf16[256,512]{1,0:T(8,128)(2,1)}, u32[]{:S(2)}, u32[]{:S(2)}) collective-permute-start(bf16[256,512]{1,0:T(8,128)(2,1)S(1)} %get-tuple-element.31), channel_id=1, source_target_pairs={{0,1},{1,2},{2,3},{3,0},{4,5},{5,6},{6,7},{7,4},{8,9},{9,10},{10,1... | collective-permute-start | bytes 786440 | tf_op jit(solution)/shard_map/ppermute | solution.py:249
  4.9 19.8 %collective-permute-start.3 = (bf16[256,512]{1,0:T(8,128)(2,1)S(1)}, bf16[256,512]{1,0:T(8,128)(2,1)}, u32[]{:S(2)}, u32[]{:S(2)}) collective-permute-start(bf16[256,512]{1,0:T(8,128)(2,1)S(1)} %get-tuple-element.31), channel_id=1, source_target_pairs={{0,2},{1,3},{2,0},{3,1},{4,6},{5,7},{6,4},{7,5},{8,10},{9,11},{10,... | collective-permute-start | bytes 786440 | tf_op jit(solution)/shard_map/ppermute | solution.py:249
  7.5 18.2 %collective-permute-start.4 = (bf16[256,512]{1,0:T(8,128)(2,1)S(1)}, bf16[256,512]{1,0:T(8,128)(2,1)}, u32[]{:S(2)}, u32[]{:S(2)}) collective-permute-start(bf16[256,512]{1,0:T(8,128)(2,1)S(1)} %get-tuple-element.31), channel_id=1, source_target_pairs={{0,3},{1,0},{2,1},{3,2},{4,7},{5,4},{6,5},{7,6},{8,11},{9,8},{10,9... | collective-permute-start | bytes 786440 | tf_op jit(solution)/shard_map/ppermute | solution.py:249
  9.6 16.2 %copy-start.10 = (bf16[512,512]{1,0:T(8,128)(2,1)}, bf16[512,512]{1,0:T(8,128)(2,1)S(1)}, u32[]{:S(2)}) copy-start(bf16[512,512]{1,0:T(8,128)(2,1)S(1)} %rev.3) | copy-start | bytes 1572868
  10.0 18.7 %copy-start.13 = (bf16[384,512]{1,0:T(8,128)(2,1)}, bf16[384,512]{1,0:T(8,128)(2,1)S(1)}, u32[]{:S(2)}) copy-start(bf16[384,512]{1,0:T(8,128)(2,1)S(1)} %get-tuple-element.54) | copy-start | bytes 1179652
  10.0 17.6 %collective-permute-start.1 = (bf16[384,512]{1,0:T(8,128)(2,1)S(1)}, bf16[384,512]{1,0:T(8,128)(2,1)}, u32[]{:S(2)}, u32[]{:S(2)}) collective-permute-start(bf16[384,512]{1,0:T(8,128)(2,1)S(1)} %get-tuple-element.54), channel_id=1, source_target_pairs={{4,0},{8,4},{12,8},{16,12},{20,16},{24,20},{28,24},{5,1},{9,5},{13... | collective-permute-start | bytes 1179656 | tf_op jit(solution)/shard_map/ppermute | solution.py:23
  11.4 17.4 %collective-permute-start = (bf16[384,512]{1,0:T(8,128)(2,1)S(1)}, bf16[384,512]{1,0:T(8,128)(2,1)S(1)}, u32[]{:S(2)}, u32[]{:S(2)}) collective-permute-start(bf16[384,512]{1,0:T(8,128)(2,1)S(1)} %slice_bitcast_fusion.10), channel_id=1, source_target_pairs={{0,4},{4,8},{8,12},{12,16},{16,20},{20,24},{24,28},{1,5},{5,9},{9,... | collective-permute-start | bytes 1179656 | tf_op jit(solution)/shard_map/ppermute | solution.py:23
  26.7 3.1 %collective-permute-start.5 = (bf16[1024,512]{1,0:T(8,128)(2,1)S(1)}, bf16[1024,512]{1,0:T(8,128)(2,1)S(1)}, u32[]{:S(2)}, u32[]{:S(2)}) collective-permute-start(bf16[1024,512]{1,0:T(8,128)(2,1)S(1)} %bitcast.117), channel_id=1, source_target_pairs={{0,4},{4,0},{8,12},{12,8},{16,20},{20,16},{24,28},{28,24},{1,5},{5... | collective-permute-start | bytes 3145736 | tf_op jit(solution)/shard_map/ppermute | solution.py:255
  28.7 0.7 copy-start.27
  29.8 0.7 copy-start.7
  30.1 16.4 %copy-start.4 = (bf16[1024,512]{1,0:T(8,128)(2,1)}, bf16[1024,512]{1,0:T(8,128)(2,1)S(1)}, u32[]{:S(2)}) copy-start(bf16[1024,512]{1,0:T(8,128)(2,1)S(1)} %get-tuple-element.32.p_ref) | copy-start | bytes 3145732
  38.8 4.0 %copy-start.26 = (bf16[1,384,1024]{2,1,0:T(8,128)(2,1)S(1)}, bf16[1,384,1024]{2,1,0:T(8,128)(2,1)}, u32[]{:S(2)}) copy-start(bf16[1,384,1024]{2,1,0:T(8,128)(2,1)} %param.13) | copy-start | bytes 2359300
  38.8 4.1 %copy-start.11 = (bf16[512,512]{1,0:T(8,128)(2,1)S(1)}, bf16[512,512]{1,0:T(8,128)(2,1)}, u32[]{:S(2)}) copy-start(bf16[512,512]{1,0:T(8,128)(2,1)} %copy-done.10) | copy-start | bytes 1572868
  38.9 4.4 %collective-permute-start.6 = (bf16[384,1024]{1,0:T(8,128)(2,1)S(1)}, bf16[384,1024]{1,0:T(8,128)(2,1)S(1)}, u32[]{:S(2)}, u32[]{:S(2)}) collective-permute-start(bf16[384,1024]{1,0:T(8,128)(2,1)S(1)} %get-tuple-element.38), channel_id=1, source_target_pairs={{0,4},{4,8},{8,12},{12,16},{16,20},{20,24},{24,28},{1,5},{5,9},{9,... | collective-permute-start | bytes 2359304 | tf_op jit(solution)/shard_map/ppermute | solution.py:23
  41.5 4.8 %collective-permute-start.7 = (bf16[384,1024]{1,0:T(8,128)(2,1)S(1)}, bf16[384,1024]{1,0:T(8,128)(2,1)S(1)}, u32[]{:S(2)}, u32[]{:S(2)}) collective-permute-start(bf16[384,1024]{1,0:T(8,128)(2,1)S(1)} %get-tuple-element.39), channel_id=1, source_target_pairs={{4,0},{8,4},{12,8},{16,12},{20,16},{24,20},{28,24},{5,1},{9,5},{13... | collective-permute-start | bytes 2359304 | tf_op jit(solution)/shard_map/ppermute | solution.py:23
  42.9 3.4 %copy-start.21 = (bf16[1,384,512]{2,1,0:T(8,128)(2,1)}, bf16[1,384,512]{2,1,0:T(8,128)(2,1)S(1)}, u32[]{:S(2)}) copy-start(bf16[1,384,512]{2,1,0:T(8,128)(2,1)S(1)} %slice.88) | copy-start | bytes 1179652
  43.3 3.0 %copy-start.24 = (bf16[1,384,512]{2,1,0:T(8,128)(2,1)}, bf16[1,384,512]{2,1,0:T(8,128)(2,1)S(1)}, u32[]{:S(2)}) copy-start(bf16[1,384,512]{2,1,0:T(8,128)(2,1)S(1)} %fusion.4) | copy-start | bytes 1179652
  59.1 1.6 copy-start.5
  60.7 1.8 copy-start
  60.7 2.2 copy-start.8
  62.9 22.8 %collective-permute-start.8 = (bf16[384,1024]{1,0:T(8,128)(2,1)}, bf16[384,1024]{1,0:T(8,128)(2,1)}, u32[]{:S(2)}, u32[]{:S(2)}) collective-permute-start(bf16[384,1024]{1,0:T(8,128)(2,1)} %get-tuple-element.36), channel_id=1, source_target_pairs={{4,0},{8,4},{12,8},{16,12},{20,16},{24,20},{28,24},{5,1},{9,5},{13... | collective-permute-start | bytes 2359304 | tf_op jit(solution)/shard_map/ppermute | solution.py:23
  64.2 21.5 %collective-permute-start.9 = (bf16[384,1024]{1,0:T(8,128)(2,1)}, bf16[384,1024]{1,0:T(8,128)(2,1)}, u32[]{:S(2)}, u32[]{:S(2)}) collective-permute-start(bf16[384,1024]{1,0:T(8,128)(2,1)} %get-tuple-element.37), channel_id=1, source_target_pairs={{0,4},{4,8},{8,12},{12,16},{16,20},{20,24},{24,28},{1,5},{5,9},{9,... | collective-permute-start | bytes 2359304 | tf_op jit(solution)/shard_map/ppermute | solution.py:23
  85.7 26.9 %copy-start.19 = (f32[768,512]{1,0:T(8,128)}, f32[768,512]{1,0:T(8,128)S(1)}, u32[]{:S(2)}) copy-start(f32[768,512]{1,0:T(8,128)S(1)} %fusion.30) | copy-start | bytes 4718596
  85.7 2.4 %copy-start.1 = (bf16[2,384,1024]{2,1,0:T(8,128)(2,1)S(1)}, bf16[2,384,1024]{2,1,0:T(8,128)(2,1)}, u32[]{:S(2)}) copy-start(bf16[2,384,1024]{2,1,0:T(8,128)(2,1)} %copy-done) | copy-start | bytes 4718596
  95.7 1.7 copy-start.2
  95.7 16.8 %copy-start.17 = (bf16[1,384,1024]{2,1,0:T(8,128)(2,1)S(1)}, bf16[1,384,1024]{2,1,0:T(8,128)(2,1)}, u32[]{:S(2)}) copy-start(bf16[1,384,1024]{2,1,0:T(8,128)(2,1)} %param.7) | copy-start | bytes 2359300
  95.7 17.7 %copy-start.22 = (bf16[1,384,512]{2,1,0:T(8,128)(2,1)S(1)}, bf16[1,384,512]{2,1,0:T(8,128)(2,1)}, u32[]{:S(2)}) copy-start(bf16[1,384,512]{2,1,0:T(8,128)(2,1)} %copy-done.21) | copy-start | bytes 1179652
  95.7 17.6 %copy-start.25 = (bf16[1,384,512]{2,1,0:T(8,128)(2,1)S(1)}, bf16[1,384,512]{2,1,0:T(8,128)(2,1)}, u32[]{:S(2)}) copy-start(bf16[1,384,512]{2,1,0:T(8,128)(2,1)} %copy-done.24) | copy-start | bytes 1179652
  97.4 16.0 %copy-start.9 = (bf16[2,384,1024]{2,1,0:T(8,128)(2,1)S(1)}, bf16[2,384,1024]{2,1,0:T(8,128)(2,1)}, u32[]{:S(2)}) copy-start(bf16[2,384,1024]{2,1,0:T(8,128)(2,1)} %copy-done.8) | copy-start | bytes 4718596
  97.4 18.4 %collective-permute-start.10 = (bf16[384,1024]{1,0:T(8,128)(2,1)}, bf16[384,1024]{1,0:T(8,128)(2,1)}, u32[]{:S(2)}, u32[]{:S(2)}) collective-permute-start(bf16[384,1024]{1,0:T(8,128)(2,1)} %get-tuple-element.34), channel_id=1, source_target_pairs={{4,0},{8,4},{12,8},{16,12},{20,16},{24,20},{28,24},{5,1},{9,5},{13... | collective-permute-start | bytes 2359304 | tf_op jit(solution)/shard_map/ppermute | solution.py:23
  98.8 17.0 %collective-permute-start.11 = (bf16[384,1024]{1,0:T(8,128)(2,1)}, bf16[384,1024]{1,0:T(8,128)(2,1)}, u32[]{:S(2)}, u32[]{:S(2)}) collective-permute-start(bf16[384,1024]{1,0:T(8,128)(2,1)} %get-tuple-element.35), channel_id=1, source_target_pairs={{0,4},{4,8},{8,12},{12,16},{16,20},{20,24},{24,28},{1,5},{5,9},{9,... | collective-permute-start | bytes 2359304 | tf_op jit(solution)/shard_map/ppermute | solution.py:23
  113.4 4.1 %copy-start.6 = (f32[2,384,1024]{2,1,0:T(8,128)S(1)}, f32[2,384,1024]{2,1,0:T(8,128)}, u32[]{:S(2)}) copy-start(f32[2,384,1024]{2,1,0:T(8,128)} %copy-done.5) | copy-start | bytes 9437188
  115.8 1.9 copy-start.3
  117.7 4.6 %copy-start.18 = (bf16[1,384,1024]{2,1,0:T(8,128)(2,1)S(1)}, bf16[1,384,1024]{2,1,0:T(8,128)(2,1)}, u32[]{:S(2)}) copy-start(bf16[1,384,1024]{2,1,0:T(8,128)(2,1)} %param.7) | copy-start | bytes 2359300
  122.3 1.0 copy-start.14
  123.3 1.6 copy-start.15
  143.1 9.4 %collective-permute-start.12 = (bf16[4,1152,128]{2,1,0:T(8,128)(2,1)S(1)}, bf16[4,1152,128]{2,1,0:T(8,128)(2,1)}, u32[]{:S(2)}, u32[]{:S(2)}) collective-permute-start(bf16[4,1152,128]{2,1,0:T(8,128)(2,1)S(1)} %select_convert_fusion), channel_id=1, source_target_pairs={{0,4},{4,0},{8,12},{12,8},{16,20},{20,16},{24,28},{28,24},{1,5},{5... | collective-permute-start | bytes 3538952 | tf_op jit(solution)/shard_map/ppermute | solution.py:255
  156.5 26.4 %collective-permute-start.13 = (bf16[4,576,128]{2,1,0:T(8,128)(2,1)}, bf16[4,576,128]{2,1,0:T(8,128)(2,1)S(1)}, u32[]{:S(2)}, u32[]{:S(2)}) collective-permute-start(bf16[4,576,128]{2,1,0:T(8,128)(2,1)} %select_convert_fusion.1), channel_id=1, source_target_pairs={{0,8},{4,12},{8,0},{12,4},{16,24},{20,28},{24,16},{28,20},{1,9},{5... | collective-permute-start | bytes 1769480 | tf_op jit(solution)/shard_map/ppermute | solution.py:255
  183.0 8.8 %collective-permute-start.14 = (bf16[4,288,128]{2,1,0:T(8,128)(2,1)S(1)}, bf16[4,288,128]{2,1,0:T(8,128)(2,1)S(1)}, u32[]{:S(2)}, u32[]{:S(2)}) collective-permute-start(bf16[4,288,128]{2,1,0:T(8,128)(2,1)S(1)} %select_convert_fusion.2), channel_id=1, source_target_pairs={{0,16},{4,20},{8,24},{12,28},{16,0},{20,4},{24,8},{28,12},{1,17},{... | collective-permute-start | bytes 884744 | tf_op jit(solution)/shard_map/ppermute | solution.py:255
  191.9 22.6 %copy-start.12 = (bf16[512,512]{1,0:T(8,128)(2,1)S(1)}, bf16[512,512]{1,0:T(8,128)(2,1)}, u32[]{:S(2)}) copy-start(bf16[512,512]{1,0:T(8,128)(2,1)} %copy-done.10) | copy-start | bytes 1572868
  191.9 22.6 %copy-start.20 = (f32[768,512]{1,0:T(8,128)S(1)}, f32[768,512]{1,0:T(8,128)}, u32[]{:S(2)}) copy-start(f32[768,512]{1,0:T(8,128)} %copy-done.19) | copy-start | bytes 4718596
  192.0 10.2 %collective-permute-start.15 = (bf16[288,128]{1,0:T(8,128)(2,1)S(1)}, bf16[288,128]{1,0:T(8,128)(2,1)S(1)}, u32[]{:S(2)}, u32[]{:S(2)}) collective-permute-start(bf16[288,128]{1,0:T(8,128)(2,1)S(1)} %get-tuple-element.48), channel_id=1, source_target_pairs={{0,1},{1,2},{2,3},{3,0},{4,5},{5,6},{6,7},{7,4},{8,9},{9,10},{10,1... | collective-permute-start | bytes 221192 | tf_op jit(solution)/shard_map/ppermute | solution.py:287
  197.2 7.3 %collective-permute-start.16 = (bf16[288,128]{1,0:T(8,128)(2,1)S(1)}, bf16[288,128]{1,0:T(8,128)(2,1)S(1)}, u32[]{:S(2)}, u32[]{:S(2)}) collective-permute-start(bf16[288,128]{1,0:T(8,128)(2,1)S(1)} %get-tuple-element.50), channel_id=1, source_target_pairs={{0,2},{1,3},{2,0},{3,1},{4,6},{5,7},{6,4},{7,5},{8,10},{9,11},{10,... | collective-permute-start | bytes 221192 | tf_op jit(solution)/shard_map/ppermute | solution.py:287
  199.7 4.9 %collective-permute-start.17 = (bf16[288,128]{1,0:T(8,128)(2,1)S(1)}, bf16[288,128]{1,0:T(8,128)(2,1)S(1)}, u32[]{:S(2)}, u32[]{:S(2)}) collective-permute-start(bf16[288,128]{1,0:T(8,128)(2,1)S(1)} %get-tuple-element.49), channel_id=1, source_target_pairs={{0,3},{1,0},{2,1},{3,2},{4,7},{5,4},{6,5},{7,6},{8,11},{9,8},{10,9... | collective-permute-start | bytes 221192 | tf_op jit(solution)/shard_map/ppermute | solution.py:287
  204.7 4.4 %collective-permute-start.18 = (bf16[288,128]{1,0:T(8,128)(2,1)S(1)}, bf16[288,128]{1,0:T(8,128)(2,1)S(1)}, u32[]{:S(2)}, u32[]{:S(2)}) collective-permute-start(bf16[288,128]{1,0:T(8,128)(2,1)S(1)} %fusion.28), channel_id=1, source_target_pairs={{0,16},{4,20},{8,24},{12,28},{16,0},{20,4},{24,8},{28,12},{1,17},{... | collective-permute-start | bytes 221192 | tf_op jit(solution)/shard_map/ppermute | solution.py:255
  209.1 5.8 %copy-start.23 = (bf16[384,512]{1,0:T(8,128)(2,1)S(1)}, bf16[384,512]{1,0:T(8,128)(2,1)}, u32[]{:S(2)}) copy-start(bf16[384,512]{1,0:T(8,128)(2,1)} %get-tuple-element.41) | copy-start | bytes 1179652
  209.2 5.2 %collective-permute-start.19 = (bf16[576,128]{1,0:T(8,128)(2,1)S(1)}, bf16[576,128]{1,0:T(8,128)(2,1)S(1)}, u32[]{:S(2)}, u32[]{:S(2)}) collective-permute-start(bf16[576,128]{1,0:T(8,128)(2,1)S(1)} %pad_maximum_fusion.7), channel_id=1, source_target_pairs={{0,8},{4,12},{8,0},{12,4},{16,24},{20,28},{24,16},{28,20},{1,9},{5... | collective-permute-start | bytes 442376 | tf_op jit(solution)/shard_map/ppermute | solution.py:255
  214.5 1.6 collective-permute-start.20
  216.3 6.9 %collective-permute-start.21 = (bf16[256,128]{1,0:T(8,128)(2,1)S(1)}, bf16[256,128]{1,0:T(8,128)(2,1)S(1)}, u32[]{:S(2)}, u32[]{:S(2)}) collective-permute-start(bf16[256,128]{1,0:T(8,128)(2,1)S(1)} %slice.123), channel_id=1, source_target_pairs={{0,1},{1,2},{2,3},{3,0},{4,5},{5,6},{6,7},{7,4},{8,9},{9,10},{10,1... | collective-permute-start | bytes 196616 | tf_op jit(solution)/shard_map/ppermute | solution.py:249
  217.5 7.8 %collective-permute-start.22 = (bf16[256,128]{1,0:T(8,128)(2,1)S(1)}, bf16[256,128]{1,0:T(8,128)(2,1)S(1)}, u32[]{:S(2)}, u32[]{:S(2)}) collective-permute-start(bf16[256,128]{1,0:T(8,128)(2,1)S(1)} %slice.123), channel_id=1, source_target_pairs={{0,2},{1,3},{2,0},{3,1},{4,6},{5,7},{6,4},{7,5},{8,10},{9,11},{10,... | collective-permute-start | bytes 196616 | tf_op jit(solution)/shard_map/ppermute | solution.py:249
  219.4 6.1 %collective-permute-start.23 = (bf16[256,128]{1,0:T(8,128)(2,1)S(1)}, bf16[256,128]{1,0:T(8,128)(2,1)S(1)}, u32[]{:S(2)}, u32[]{:S(2)}) collective-permute-start(bf16[256,128]{1,0:T(8,128)(2,1)S(1)} %slice.123), channel_id=1, source_target_pairs={{0,3},{1,0},{2,1},{3,2},{4,7},{5,4},{6,5},{7,6},{8,11},{9,8},{10,9... | collective-permute-start | bytes 196616 | tf_op jit(solution)/shard_map/ppermute | solution.py:249

commit v2 on v1

--- a/solution.py
+++ b/solution.py
@@ -272,8 +272,7 @@
     bits = lax.axis_size("ctx").bit_length() - 1
     cols = taps.reshape(count, taps.shape[2]).T
     packed = jnp.concatenate([grad_in, grad_out, jnp.pad(cols, ((0, 0), (0, 128 - count)))], axis=1)
-    groups = packed.shape[1] // 128
-    x = packed.reshape(owners, per, groups, 128).transpose(0, 2, 1, 3).reshape(owners, groups * per, 128)
+    x = packed.reshape(owners, per, packed.shape[1])
     for bit in range(bits):
         upper = (me >> bit) % 2 == 1
         middle = x.shape[1] // 2
@@ -291,11 +290,9 @@
         upper = (me >> bit) % 2 == 1
         got = swapped(x, bit)
         x = jnp.concatenate([jnp.where(upper, got, x), jnp.where(upper, x, got)], axis=0)
-    x = x.reshape(groups, per, 128)
-    wide = x[:-1].transpose(1, 0, 2).reshape(per, 2 * half)
-    tap_rows = gathered(x[-1], "fsdp")
+    tap_rows = gathered(x[:, 2 * half :], "fsdp")
     grad_taps = tap_rows[:, :count].T.reshape(taps.shape)
-    return wide[:, :half].astype(F32), wide[:, half:].astype(F32), grad_taps.astype(F32)
+    return x[:, :half].astype(F32), x[:, half : 2 * half].astype(F32), grad_taps.astype(F32)
 
 
 def solution(mesh):

time: 229 us -> 221 us (0.965)
  local copies, waits for them, and re-layouts: 30.4 us -> 21.2 us
    reshape x2 -> x1, local copies, waits for them, and re-layouts: 13.1 us -> 6.1 us  [summed(): x = packed.reshape(owners, per, packed.shape[1])]
    unnamed x61 -> x59, local copies, waits for them, and re-layouts: 8.35 us -> 6.37 us
  transfers between devices with their start and end apart: 24 -> 24, of which waited for: 13 -> 13; matrix products, arithmetic and copies ran while one was open for 8% -> 7% of each run, Pallas kernels for 0% -> 0%
where the time goes in v2:
time: 221 us
  starting transfers between devices  86.4 us (39%)
  waiting for transfers between devices  51.3 us (23%)
  Pallas kernels  32.9 us (15%)
  local copies, waits for them, and re-layouts  21.2 us (10%)
  other arithmetic  19.9 us (9%)
  matrix products  7.91 us (4%)
    ppermute x8, starting transfers between devices, passed_along(): return lax.ppermute(value, axis, pairs)  43.4 us
    pallas_call x4, Pallas kernels, call(): pl.pallas_call(kernel, grid=(inner // BLOCK,), in_specs=specs + in_specs,...  32.9 us
    ppermute x7, waiting for transfers between devices, swapped(): lax.ppermute(x, 'ctx', [(i, i ^ 1 << bit) for i in range(lax.axis_size('c...  30.1 us
    ppermute x7, starting transfers between devices, swapped(): lax.ppermute(x, 'ctx', [(i, i ^ 1 << bit) for i in range(lax.axis_size('c...  24.3 us
    ppermute x6, waiting for transfers between devices, gathered(): got = lax.ppermute(x, axis, [(i, (i + k) % n) for i in range(n)])  13.4 us
    ppermute x6, starting transfers between devices, gathered(): got = lax.ppermute(x, axis, [(i, (i + k) % n) for i in range(n)])  10.9 us
    dot_general x7, matrix products, mm(): return lax.dot_general(a, b, (dims, ((), ())), preferred_element_type=F32)  7.91 us
    ppermute x3, starting transfers between devices, summed(): lax.ppermute(piece, 'fsdp', [(i, (i + k) % owners) for i in range(owners)])  7.77 us
  transfers between devices with their start and end apart: 24, of which 13 were waited for; matrix products, arithmetic and copies ran while one was open for 7% of the time, Pallas kernels for 0%

profile of v2, /device:TPU:0, one launch (start us, length us, event | category | flops | bytes accessed | tf_op | source)
XLA Modules:
  0.0 221.1 jit_solution(15221912887692835463)
XLA Ops:
  0.7 1.1 bitcast_dynamic-update-slice_fusion.3
  1.8 3.1 %collective-permute-start.2 = (bf16[256,512]{1,0:T(8,128)(2,1)S(1)}, bf16[256,512]{1,0:T(8,128)(2,1)}, u32[]{:S(2)}, u32[]{:S(2)}) collective-permute-start(bf16[256,512]{1,0:T(8,128)(2,1)S(1)} %get-tuple-element.33), channel_id=1, source_target_pairs={{0,1},{1,2},{2,3},{3,0},{4,5},{5,6},{6,7},{7,4},{8,9},{9,10},{10,1... | collective-permute-start | bytes 786440 | tf_op jit(solution)/shard_map/ppermute | solution.py:249
  4.9 2.6 %collective-permute-start.3 = (bf16[256,512]{1,0:T(8,128)(2,1)S(1)}, bf16[256,512]{1,0:T(8,128)(2,1)}, u32[]{:S(2)}, u32[]{:S(2)}) collective-permute-start(bf16[256,512]{1,0:T(8,128)(2,1)S(1)} %get-tuple-element.33), channel_id=1, source_target_pairs={{0,2},{1,3},{2,0},{3,1},{4,6},{5,7},{6,4},{7,5},{8,10},{9,11},{10,... | collective-permute-start | bytes 786440 | tf_op jit(solution)/shard_map/ppermute | solution.py:249
  7.5 1.3 collective-permute-start.4
  8.9 0.6 rev.3
  9.6 0.5 fusion.9
  10.0 1.3 collective-permute-start.1
  11.4 3.1 %collective-permute-start = (bf16[384,512]{1,0:T(8,128)(2,1)S(1)}, bf16[384,512]{1,0:T(8,128)(2,1)S(1)}, u32[]{:S(2)}, u32[]{:S(2)}) collective-permute-start(bf16[384,512]{1,0:T(8,128)(2,1)S(1)} %slice_bitcast_fusion.10), channel_id=1, source_target_pairs={{0,4},{4,8},{8,12},{12,16},{16,20},{20,24},{24,28},{1,5},{5,9},{9,... | collective-permute-start | bytes 1179656 | tf_op jit(solution)/shard_map/ppermute | solution.py:23
  14.5 1.0 bitcast_dynamic-update-slice_fusion.2
  15.5 9.3 %collective-permute-done.3 = bf16[256,512]{1,0:T(8,128)(2,1)} collective-permute-done((bf16[256,512]{1,0:T(8,128)(2,1)S(1)}, bf16[256,512]{1,0:T(8,128)(2,1)}, u32[]{:S(2)}, u32[]{:S(2)}) %collective-permute-start.3) | collective-permute-done | bytes 262176 | tf_op jit(solution)/shard_map/ppermute | solution.py:249
  24.7 1.0 bitcast_dynamic-update-slice_fusion.1
  25.7 1.0 bitcast_dynamic-update-slice_fusion
  26.8 0.8 copy.43.w_ref
  27.6 1.0 maximum_bitcast_fusion.1
  30.5 8.7 %shard_map.102 = (bf16[2,768,1024]{2,1,0:T(8,128)(2,1)S(1)}, bf16[2,384,1024]{2,1,0:T(8,128)(2,1)S(1)}) custom-call(s32[2]{0:T(128)S(1)} %copy-done.7, f32[2,7,1024]{2,1,0:T(8,128)S(1)} %copy.43.w_ref, bf16[2,768,512]{2,1,0:T(8,128)(2,1)S(1)} %fusion.2.n_ref, bf16[1024,512]{1,0:T(8,128)(2,1)S(1)} %get-tuple-element.35.p_ref), custom_call_target="tpu_custom_call" | custom-call | flops 2000000000 | bytes 8388608 | tf_op jit(solution)/shard_map/pallas_call | solution.py:161
  39.4 2.6 %collective-permute-start.6 = (bf16[384,1024]{1,0:T(8,128)(2,1)S(1)}, bf16[384,1024]{1,0:T(8,128)(2,1)S(1)}, u32[]{:S(2)}, u32[]{:S(2)}) collective-permute-start(bf16[384,1024]{1,0:T(8,128)(2,1)S(1)} %get-tuple-element.40), channel_id=1, source_target_pairs={{0,4},{4,8},{8,12},{12,16},{16,20},{20,24},{24,28},{1,5},{5,9},{9,... | collective-permute-start | bytes 2359304 | tf_op jit(solution)/shard_map/ppermute | solution.py:23
  42.0 1.3 collective-permute-start.7
  43.8 2.9 %collective-permute-done.7 = bf16[384,1024]{1,0:T(8,128)(2,1)S(1)} collective-permute-done((bf16[384,1024]{1,0:T(8,128)(2,1)S(1)}, bf16[384,1024]{1,0:T(8,128)(2,1)S(1)}, u32[]{:S(2)}, u32[]{:S(2)}) %collective-permute-start.7) | collective-permute-done | bytes 786464 | tf_op jit(solution)/shard_map/ppermute | solution.py:23
  46.9 11.7 %shard_map.103 = (bf16[2,384,1024]{2,1,0:T(8,128)(2,1)S(1)}, bf16[2,384,1024]{2,1,0:T(8,128)(2,1)S(1)}, f32[2,384,1024]{2,1,0:T(8,128)S(1)}, f32[7,1024]{1,0:T(8,128)S(1)}) custom-call(s32[2]{0:T(128)S(1)} %copy-done.7, f32[2,7,1024]{2,1,0:T(8,128)S(1)} %copy.43.w_ref, bf16[2,384,1024]{2,1,0:T(8,128)(2,1)S(1)} %get-tuple-element.12.f_ref, ...), custom_call_target="tpu_custom_call" | custom-call | flops 2000000000 | bytes 8388608 | tf_op jit(solution)/shard_map/pallas_call | solution.py:161
  58.6 1.6 copy-done.5
  60.2 1.5 slice_bitcast_fusion.7
  62.5 1.3 collective-permute-start.8
  63.7 18.7 %collective-permute-start.9 = (bf16[384,1024]{1,0:T(8,128)(2,1)}, bf16[384,1024]{1,0:T(8,128)(2,1)}, u32[]{:S(2)}, u32[]{:S(2)}) collective-permute-start(bf16[384,1024]{1,0:T(8,128)(2,1)} %get-tuple-element.39), channel_id=1, source_target_pairs={{0,4},{4,8},{8,12},{12,16},{16,20},{20,24},{24,28},{1,5},{5,9},{9,... | collective-permute-start | bytes 2359304 | tf_op jit(solution)/shard_map/ppermute | solution.py:23
  82.5 2.7 %fusion.34 = f32[768,512]{1,0:T(8,128)S(1)} fusion(bf16[768,1024]{1,0:T(8,128)(2,1)} %bitcast.106, bf16[1024,512]{1,0:T(8,128)(2,1)} %copy-done.4), kind=kOutput, calls=%fused_computation.102 | convolution fusion | flops 805306368 | bytes 4194304 | tf_op jit(solution)/shard_map/dot_general | solution.py:33
  85.2 2.1 pad_maximum_fusion.2.rim_ref
  87.7 7.5 %shard_map.104 = (bf16[2,384,1024]{2,1,0:T(8,128)(2,1)S(1)}, f32[7,1024]{1,0:T(8,128)S(1)}) custom-call(s32[2]{0:T(128)S(1)} %copy-done.7, f32[2,7,1024]{2,1,0:T(8,128)S(1)} %copy.43.w_ref, bf16[2,384,1024]{2,1,0:T(8,128)(2,1)S(1)} %copy-done.1, bf16[2,384,1024]{2,1,0:T(8,128)(2,1)S(1)} %pad_maximum_fusion.2.rim_ref, ...), custom_call_target="tpu_custom_call" | custom-call | flops 1000000000 | bytes 8388608 | tf_op jit(solution)/shard_map/pallas_call | solution.py:161
  95.3 1.3 slice_bitcast_fusion.5
  96.9 1.4 collective-permute-start.10
  98.3 13.7 %collective-permute-start.11 = (bf16[384,1024]{1,0:T(8,128)(2,1)}, bf16[384,1024]{1,0:T(8,128)(2,1)}, u32[]{:S(2)}, u32[]{:S(2)}) collective-permute-start(bf16[384,1024]{1,0:T(8,128)(2,1)} %get-tuple-element.37), channel_id=1, source_target_pairs={{0,4},{4,8},{8,12},{12,16},{16,20},{20,24},{24,28},{1,5},{5,9},{9,... | collective-permute-start | bytes 2359304 | tf_op jit(solution)/shard_map/ppermute | solution.py:23
  112.0 0.9 fusion.7
  112.9 2.4 %convolution_bitcast_fusion = f32[1024,512]{0,1:T(8,128)} fusion(bf16[2,384,1024]{2,1,0:T(8,128)(2,1)S(1)} %copy-done.9, bf16[1,384,512]{2,1,0:T(8,128)(2,1)S(1)} %copy-done.25, bf16[1,384,512]{2,1,0:T(8,128)(2,1)S(1)} %copy-done.22), kind=kOutput, calls=%fused_computation.10 | convolution fusion | flops 805699584 | bytes 4456448 | tf_op jit(solution)/shard_map/dot_general | solution.py:33
  115.3 1.6 pad_maximum_fusion.3.rim_ref
  117.2 4.9 %shard_map.105 = bf16[2,384,1024]{2,1,0:T(8,128)(2,1)S(1)} custom-call(s32[2]{0:T(128)S(1)} %copy-done.7, f32[2,7,1024]{2,1,0:T(8,128)S(1)} %copy.43.w_ref, bf16[2,384,1024]{2,1,0:T(8,128)(2,1)S(1)} %copy-done.3, bf16[2,384,1024]{2,1,0:T(8,128)(2,1)S(1)} %pad_maximum_fusion.3.rim_ref, f32[2,384,1024]{2,1,0:T(8,128)S(1)} %copy-done.6), custom_call_target="tpu_custom_call" | custom-call | flops 1000000000 | bytes 8388608 | tf_op jit(solution)/shard_map/pallas_call | solution.py:161
  122.2 0.8 fusion.12
  123.2 0.8 convolution_add_fusion
  124.0 0.7 copy-done.15
  124.7 2.6 %select_maximum_fusion = f32[1024,1152]{0,1:T(8,128)} fusion(f32[1024,14]{0,1:T(8,128)S(1)} %bitcast.114, f32[1024,512]{0,1:T(8,128)S(1)} %copy-done.15, f32[1024,512]{0,1:T(8,128)S(1)} %convolution_add_fusion), kind=kLoop, calls=%fused_computation | loop fusion | flops 4718592 | bytes 8970240 | tf_op jit(solution)/shard_map/concatenate | solution.py:274
  127.3 6.1 %copy.58 = f32[1024,1152]{1,0:T(8,128)} copy(f32[1024,1152]{0,1:T(8,128)} %select_maximum_fusion) | data formatting | bytes 9437184 | tf_op jit(solution)/shard_map/reshape | solution.py:275
  133.4 2.6 %select_convert_fusion = bf16[4,128,1152]{2,1,0:T(8,128)(2,1)S(1)} fusion(f32[4,256,1152]{2,1,0:T(8,128)} %bitcast.107, pred[]{:T(512)S(6)} %eq.37), kind=kLoop, calls=%fused_computation.8 | loop fusion | flops 589824 | bytes 3538945 | tf_op jit(solution)/shard_map/convert_element_type | solution.py:280
  136.0 6.8 %collective-permute-start.12 = (bf16[4,128,1152]{2,1,0:T(8,128)(2,1)S(1)}, bf16[4,128,1152]{2,1,0:T(8,128)(2,1)}, u32[]{:S(2)}, u32[]{:S(2)}) collective-permute-start(bf16[4,128,1152]{2,1,0:T(8,128)(2,1)S(1)} %select_convert_fusion), channel_id=1, source_target_pairs={{0,4},{4,0},{8,12},{12,8},{16,20},{20,16},{24,28},{28,24},{1,5},{5... | collective-permute-start | bytes 3538952 | tf_op jit(solution)/shard_map/ppermute | solution.py:255
  142.8 2.6 %collective-permute-done.12 = bf16[4,128,1152]{2,1,0:T(8,128)(2,1)} collective-permute-done((bf16[4,128,1152]{2,1,0:T(8,128)(2,1)S(1)}, bf16[4,128,1152]{2,1,0:T(8,128)(2,1)}, u32[]{:S(2)}, u32[]{:S(2)}) %collective-permute-start.12) | collective-permute-done | bytes 1179680 | tf_op jit(solution)/shard_map/ppermute | solution.py:255
  145.4 3.0 %convert_add_fusion = f32[4,128,1152]{2,1,0:T(8,128)S(1)} fusion(bf16[4,128,1152]{2,1,0:T(8,128)(2,1)} %collective-permute-done.12, f32[4,256,1152]{2,1,0:T(8,128)} %bitcast.108, pred[]{:T(512)S(6)} %eq.37), kind=kLoop, calls=%fused_computation.7 | loop fusion | flops 1769472 | bytes 8257537 | tf_op jit(solution)/shard_map/add | solution.py:281
  148.4 0.9 select_convert_fusion.1
  149.4 12.3 %collective-permute-start.13 = (bf16[4,64,1152]{2,1,0:T(8,128)(2,1)}, bf16[4,64,1152]{2,1,0:T(8,128)(2,1)S(1)}, u32[]{:S(2)}, u32[]{:S(2)}) collective-permute-start(bf16[4,64,1152]{2,1,0:T(8,128)(2,1)} %select_convert_fusion.1), channel_id=1, source_target_pairs={{0,8},{4,12},{8,0},{12,4},{16,24},{20,28},{24,16},{28,20},{1,9},{5... | collective-permute-start | bytes 1769480 | tf_op jit(solution)/shard_map/ppermute | solution.py:255
  161.7 14.1 %collective-permute-done.13 = bf16[4,64,1152]{2,1,0:T(8,128)(2,1)S(1)} collective-permute-done((bf16[4,64,1152]{2,1,0:T(8,128)(2,1)}, bf16[4,64,1152]{2,1,0:T(8,128)(2,1)S(1)}, u32[]{:S(2)}, u32[]{:S(2)}) %collective-permute-start.13) | collective-permute-done | bytes 589856 | tf_op jit(solution)/shard_map/ppermute | solution.py:255
  176.0 1.9 collective-permute-start.14
  177.9 6.8 %collective-permute-done.14 = bf16[4,32,1152]{2,1,0:T(8,128)(2,1)S(1)} collective-permute-done((bf16[4,32,1152]{2,1,0:T(8,128)(2,1)S(1)}, bf16[4,32,1152]{2,1,0:T(8,128)(2,1)S(1)}, u32[]{:S(2)}, u32[]{:S(2)}) %collective-permute-start.14) | collective-permute-done | bytes 294944 | tf_op jit(solution)/shard_map/ppermute | solution.py:255
  184.9 5.2 %collective-permute-start.15 = (bf16[32,1152]{1,0:T(8,128)(2,1)S(1)}, bf16[32,1152]{1,0:T(8,128)(2,1)S(1)}, u32[]{:S(2)}, u32[]{:S(2)}) collective-permute-start(bf16[32,1152]{1,0:T(8,128)(2,1)S(1)} %get-tuple-element.50), channel_id=1, source_target_pairs={{0,1},{1,2},{2,3},{3,0},{4,5},{5,6},{6,7},{7,4},{8,9},{9,10},{10,1... | collective-permute-start | bytes 221192 | tf_op jit(solution)/shard_map/ppermute | solution.py:286
  190.1 2.6 %collective-permute-start.16 = (bf16[32,1152]{1,0:T(8,128)(2,1)S(1)}, bf16[32,1152]{1,0:T(8,128)(2,1)S(1)}, u32[]{:S(2)}, u32[]{:S(2)}) collective-permute-start(bf16[32,1152]{1,0:T(8,128)(2,1)S(1)} %get-tuple-element.52), channel_id=1, source_target_pairs={{0,2},{1,3},{2,0},{3,1},{4,6},{5,7},{6,4},{7,5},{8,10},{9,11},{10,... | collective-permute-start | bytes 221192 | tf_op jit(solution)/shard_map/ppermute | solution.py:286
  192.7 2.5 %collective-permute-done.15 = bf16[32,1152]{1,0:T(8,128)(2,1)S(1)} collective-permute-done((bf16[32,1152]{1,0:T(8,128)(2,1)S(1)}, bf16[32,1152]{1,0:T(8,128)(2,1)S(1)}, u32[]{:S(2)}, u32[]{:S(2)}) %collective-permute-start.15) | collective-permute-done | bytes 73760 | tf_op jit(solution)/shard_map/ppermute | solution.py:286
  195.2 2.2 collective-permute-done.16
  197.6 1.7 collective-permute-start.18
  199.3 2.7 %collective-permute-done.18 = bf16[32,1152]{1,0:T(8,128)(2,1)S(1)} collective-permute-done((bf16[32,1152]{1,0:T(8,128)(2,1)S(1)}, bf16[32,1152]{1,0:T(8,128)(2,1)S(1)}, u32[]{:S(2)}, u32[]{:S(2)}) %collective-permute-start.18) | collective-permute-done | bytes 73760 | tf_op jit(solution)/shard_map/ppermute | solution.py:255
  202.1 1.5 collective-permute-start.19
  203.6 3.7 %collective-permute-done.19 = bf16[64,1152]{1,0:T(8,128)(2,1)S(1)} collective-permute-done((bf16[64,1152]{1,0:T(8,128)(2,1)S(1)}, bf16[64,1152]{1,0:T(8,128)(2,1)S(1)}, u32[]{:S(2)}, u32[]{:S(2)}) %collective-permute-start.19) | collective-permute-done | bytes 147488 | tf_op jit(solution)/shard_map/ppermute | solution.py:255
  207.9 1.0 maximum_bitcast_fusion.2
  209.2 1.2 collective-permute-start.21
  210.5 1.9 collective-permute-start.22
  212.4 0.7 collective-permute-start.23
  213.1 1.1 fusion.27
  214.2 1.9 collective-permute-done.21
  216.1 2.2 collective-permute-done.22
  218.7 1.7 dynamic_update_slice.31
  220.4 0.7 copy.53
  (107 shorter events, 6.5 us)
Async XLA Ops:
  0.7 8.8 %copy-start.16 = (bf16[1,384,1024]{2,1,0:T(8,128)(2,1)S(1)}, bf16[1,384,1024]{2,1,0:T(8,128)(2,1)}, u32[]{:S(2)}) copy-start(bf16[1,384,1024]{2,1,0:T(8,128)(2,1)} %param.7) | copy-start | bytes 2359300
  1.8 12.6 %collective-permute-start.2 = (bf16[256,512]{1,0:T(8,128)(2,1)S(1)}, bf16[256,512]{1,0:T(8,128)(2,1)}, u32[]{:S(2)}, u32[]{:S(2)}) collective-permute-start(bf16[256,512]{1,0:T(8,128)(2,1)S(1)} %get-tuple-element.33), channel_id=1, source_target_pairs={{0,1},{1,2},{2,3},{3,0},{4,5},{5,6},{6,7},{7,4},{8,9},{9,10},{10,1... | collective-permute-start | bytes 786440 | tf_op jit(solution)/shard_map/ppermute | solution.py:249
  4.9 19.8 %collective-permute-start.3 = (bf16[256,512]{1,0:T(8,128)(2,1)S(1)}, bf16[256,512]{1,0:T(8,128)(2,1)}, u32[]{:S(2)}, u32[]{:S(2)}) collective-permute-start(bf16[256,512]{1,0:T(8,128)(2,1)S(1)} %get-tuple-element.33), channel_id=1, source_target_pairs={{0,2},{1,3},{2,0},{3,1},{4,6},{5,7},{6,4},{7,5},{8,10},{9,11},{10,... | collective-permute-start | bytes 786440 | tf_op jit(solution)/shard_map/ppermute | solution.py:249
  7.5 18.2 %collective-permute-start.4 = (bf16[256,512]{1,0:T(8,128)(2,1)S(1)}, bf16[256,512]{1,0:T(8,128)(2,1)}, u32[]{:S(2)}, u32[]{:S(2)}) collective-permute-start(bf16[256,512]{1,0:T(8,128)(2,1)S(1)} %get-tuple-element.33), channel_id=1, source_target_pairs={{0,3},{1,0},{2,1},{3,2},{4,7},{5,4},{6,5},{7,6},{8,11},{9,8},{10,9... | collective-permute-start | bytes 786440 | tf_op jit(solution)/shard_map/ppermute | solution.py:249
  9.6 16.2 %copy-start.10 = (bf16[512,512]{1,0:T(8,128)(2,1)}, bf16[512,512]{1,0:T(8,128)(2,1)S(1)}, u32[]{:S(2)}) copy-start(bf16[512,512]{1,0:T(8,128)(2,1)S(1)} %rev.3) | copy-start | bytes 1572868
  10.0 18.7 %copy-start.13 = (bf16[384,512]{1,0:T(8,128)(2,1)}, bf16[384,512]{1,0:T(8,128)(2,1)S(1)}, u32[]{:S(2)}) copy-start(bf16[384,512]{1,0:T(8,128)(2,1)S(1)} %get-tuple-element.56) | copy-start | bytes 1179652
  10.0 17.6 %collective-permute-start.1 = (bf16[384,512]{1,0:T(8,128)(2,1)S(1)}, bf16[384,512]{1,0:T(8,128)(2,1)}, u32[]{:S(2)}, u32[]{:S(2)}) collective-permute-start(bf16[384,512]{1,0:T(8,128)(2,1)S(1)} %get-tuple-element.56), channel_id=1, source_target_pairs={{4,0},{8,4},{12,8},{16,12},{20,16},{24,20},{28,24},{5,1},{9,5},{13... | collective-permute-start | bytes 1179656 | tf_op jit(solution)/shard_map/ppermute | solution.py:23
  11.4 17.4 %collective-permute-start = (bf16[384,512]{1,0:T(8,128)(2,1)S(1)}, bf16[384,512]{1,0:T(8,128)(2,1)S(1)}, u32[]{:S(2)}, u32[]{:S(2)}) collective-permute-start(bf16[384,512]{1,0:T(8,128)(2,1)S(1)} %slice_bitcast_fusion.10), channel_id=1, source_target_pairs={{0,4},{4,8},{8,12},{12,16},{16,20},{20,24},{24,28},{1,5},{5,9},{9,... | collective-permute-start | bytes 1179656 | tf_op jit(solution)/shard_map/ppermute | solution.py:23
  26.7 3.1 %collective-permute-start.5 = (bf16[1024,512]{1,0:T(8,128)(2,1)S(1)}, bf16[1024,512]{1,0:T(8,128)(2,1)S(1)}, u32[]{:S(2)}, u32[]{:S(2)}) collective-permute-start(bf16[1024,512]{1,0:T(8,128)(2,1)S(1)} %bitcast.109), channel_id=1, source_target_pairs={{0,4},{4,0},{8,12},{12,8},{16,20},{20,16},{24,28},{28,24},{1,5},{5... | collective-permute-start | bytes 3145736 | tf_op jit(solution)/shard_map/ppermute | solution.py:255
  28.7 0.7 copy-start.27
  29.8 0.7 copy-start.7
  30.1 16.8 %copy-start.4 = (bf16[1024,512]{1,0:T(8,128)(2,1)}, bf16[1024,512]{1,0:T(8,128)(2,1)S(1)}, u32[]{:S(2)}) copy-start(bf16[1024,512]{1,0:T(8,128)(2,1)S(1)} %get-tuple-element.34.p_ref) | copy-start | bytes 3145732
  39.2 4.0 %copy-start.26 = (bf16[1,384,1024]{2,1,0:T(8,128)(2,1)S(1)}, bf16[1,384,1024]{2,1,0:T(8,128)(2,1)}, u32[]{:S(2)}) copy-start(bf16[1,384,1024]{2,1,0:T(8,128)(2,1)} %param.13) | copy-start | bytes 2359300
  39.2 4.1 %copy-start.11 = (bf16[512,512]{1,0:T(8,128)(2,1)S(1)}, bf16[512,512]{1,0:T(8,128)(2,1)}, u32[]{:S(2)}) copy-start(bf16[512,512]{1,0:T(8,128)(2,1)} %copy-done.10) | copy-start | bytes 1572868
  39.4 4.4 %collective-permute-start.6 = (bf16[384,1024]{1,0:T(8,128)(2,1)S(1)}, bf16[384,1024]{1,0:T(8,128)(2,1)S(1)}, u32[]{:S(2)}, u32[]{:S(2)}) collective-permute-start(bf16[384,1024]{1,0:T(8,128)(2,1)S(1)} %get-tuple-element.40), channel_id=1, source_target_pairs={{0,4},{4,8},{8,12},{12,16},{16,20},{20,24},{24,28},{1,5},{5,9},{9,... | collective-permute-start | bytes 2359304 | tf_op jit(solution)/shard_map/ppermute | solution.py:23
  42.0 4.8 %collective-permute-start.7 = (bf16[384,1024]{1,0:T(8,128)(2,1)S(1)}, bf16[384,1024]{1,0:T(8,128)(2,1)S(1)}, u32[]{:S(2)}, u32[]{:S(2)}) collective-permute-start(bf16[384,1024]{1,0:T(8,128)(2,1)S(1)} %get-tuple-element.41), channel_id=1, source_target_pairs={{4,0},{8,4},{12,8},{16,12},{20,16},{24,20},{28,24},{5,1},{9,5},{13... | collective-permute-start | bytes 2359304 | tf_op jit(solution)/shard_map/ppermute | solution.py:23
  43.3 3.4 %copy-start.21 = (bf16[1,384,512]{2,1,0:T(8,128)(2,1)}, bf16[1,384,512]{2,1,0:T(8,128)(2,1)S(1)}, u32[]{:S(2)}) copy-start(bf16[1,384,512]{2,1,0:T(8,128)(2,1)S(1)} %slice.78) | copy-start | bytes 1179652
  43.7 3.0 %copy-start.24 = (bf16[1,384,512]{2,1,0:T(8,128)(2,1)}, bf16[1,384,512]{2,1,0:T(8,128)(2,1)S(1)}, u32[]{:S(2)}) copy-start(bf16[1,384,512]{2,1,0:T(8,128)(2,1)S(1)} %fusion.4) | copy-start | bytes 1179652
  58.6 1.6 copy-start.5
  60.2 1.8 copy-start
  60.2 2.2 %copy-start.8 = (bf16[2,384,1024]{2,1,0:T(8,128)(2,1)}, bf16[2,384,1024]{2,1,0:T(8,128)(2,1)S(1)}, u32[]{:S(2)}) copy-start(bf16[2,384,1024]{2,1,0:T(8,128)(2,1)S(1)} %get-tuple-element.14) | copy-start | bytes 4718596
  62.5 22.7 %collective-permute-start.8 = (bf16[384,1024]{1,0:T(8,128)(2,1)}, bf16[384,1024]{1,0:T(8,128)(2,1)}, u32[]{:S(2)}, u32[]{:S(2)}) collective-permute-start(bf16[384,1024]{1,0:T(8,128)(2,1)} %get-tuple-element.38), channel_id=1, source_target_pairs={{4,0},{8,4},{12,8},{16,12},{20,16},{24,20},{28,24},{5,1},{9,5},{13... | collective-permute-start | bytes 2359304 | tf_op jit(solution)/shard_map/ppermute | solution.py:23
  63.7 21.5 %collective-permute-start.9 = (bf16[384,1024]{1,0:T(8,128)(2,1)}, bf16[384,1024]{1,0:T(8,128)(2,1)}, u32[]{:S(2)}, u32[]{:S(2)}) collective-permute-start(bf16[384,1024]{1,0:T(8,128)(2,1)} %get-tuple-element.39), channel_id=1, source_target_pairs={{0,4},{4,8},{8,12},{12,16},{16,20},{20,24},{24,28},{1,5},{5,9},{9,... | collective-permute-start | bytes 2359304 | tf_op jit(solution)/shard_map/ppermute | solution.py:23
  85.2 26.8 %copy-start.19 = (f32[768,512]{1,0:T(8,128)}, f32[768,512]{1,0:T(8,128)S(1)}, u32[]{:S(2)}) copy-start(f32[768,512]{1,0:T(8,128)S(1)} %fusion.34) | copy-start | bytes 4718596
  85.2 2.4 %copy-start.1 = (bf16[2,384,1024]{2,1,0:T(8,128)(2,1)S(1)}, bf16[2,384,1024]{2,1,0:T(8,128)(2,1)}, u32[]{:S(2)}) copy-start(bf16[2,384,1024]{2,1,0:T(8,128)(2,1)} %copy-done) | copy-start | bytes 4718596
  95.2 1.7 copy-start.2
  95.2 16.8 %copy-start.17 = (bf16[1,384,1024]{2,1,0:T(8,128)(2,1)S(1)}, bf16[1,384,1024]{2,1,0:T(8,128)(2,1)}, u32[]{:S(2)}) copy-start(bf16[1,384,1024]{2,1,0:T(8,128)(2,1)} %param.7) | copy-start | bytes 2359300
  95.2 17.6 %copy-start.22 = (bf16[1,384,512]{2,1,0:T(8,128)(2,1)S(1)}, bf16[1,384,512]{2,1,0:T(8,128)(2,1)}, u32[]{:S(2)}) copy-start(bf16[1,384,512]{2,1,0:T(8,128)(2,1)} %copy-done.21) | copy-start | bytes 1179652
  95.2 17.6 %copy-start.25 = (bf16[1,384,512]{2,1,0:T(8,128)(2,1)S(1)}, bf16[1,384,512]{2,1,0:T(8,128)(2,1)}, u32[]{:S(2)}) copy-start(bf16[1,384,512]{2,1,0:T(8,128)(2,1)} %copy-done.24) | copy-start | bytes 1179652
  96.9 16.0 %copy-start.9 = (bf16[2,384,1024]{2,1,0:T(8,128)(2,1)S(1)}, bf16[2,384,1024]{2,1,0:T(8,128)(2,1)}, u32[]{:S(2)}) copy-start(bf16[2,384,1024]{2,1,0:T(8,128)(2,1)} %copy-done.8) | copy-start | bytes 4718596
  96.9 18.4 %collective-permute-start.10 = (bf16[384,1024]{1,0:T(8,128)(2,1)}, bf16[384,1024]{1,0:T(8,128)(2,1)}, u32[]{:S(2)}, u32[]{:S(2)}) collective-permute-start(bf16[384,1024]{1,0:T(8,128)(2,1)} %get-tuple-element.36), channel_id=1, source_target_pairs={{4,0},{8,4},{12,8},{16,12},{20,16},{24,20},{28,24},{5,1},{9,5},{13... | collective-permute-start | bytes 2359304 | tf_op jit(solution)/shard_map/ppermute | solution.py:23
  98.3 17.0 %collective-permute-start.11 = (bf16[384,1024]{1,0:T(8,128)(2,1)}, bf16[384,1024]{1,0:T(8,128)(2,1)}, u32[]{:S(2)}, u32[]{:S(2)}) collective-permute-start(bf16[384,1024]{1,0:T(8,128)(2,1)} %get-tuple-element.37), channel_id=1, source_target_pairs={{0,4},{4,8},{8,12},{12,16},{16,20},{20,24},{24,28},{1,5},{5,9},{9,... | collective-permute-start | bytes 2359304 | tf_op jit(solution)/shard_map/ppermute | solution.py:23
  112.9 4.1 %copy-start.6 = (f32[2,384,1024]{2,1,0:T(8,128)S(1)}, f32[2,384,1024]{2,1,0:T(8,128)}, u32[]{:S(2)}) copy-start(f32[2,384,1024]{2,1,0:T(8,128)} %copy-done.5) | copy-start | bytes 9437188
  115.3 1.9 copy-start.3
  117.2 5.0 %copy-start.18 = (bf16[1,384,1024]{2,1,0:T(8,128)(2,1)S(1)}, bf16[1,384,1024]{2,1,0:T(8,128)(2,1)}, u32[]{:S(2)}) copy-start(bf16[1,384,1024]{2,1,0:T(8,128)(2,1)} %param.7) | copy-start | bytes 2359300
  122.2 1.0 copy-start.14
  123.2 1.6 copy-start.15
  136.0 9.4 %collective-permute-start.12 = (bf16[4,128,1152]{2,1,0:T(8,128)(2,1)S(1)}, bf16[4,128,1152]{2,1,0:T(8,128)(2,1)}, u32[]{:S(2)}, u32[]{:S(2)}) collective-permute-start(bf16[4,128,1152]{2,1,0:T(8,128)(2,1)S(1)} %select_convert_fusion), channel_id=1, source_target_pairs={{0,4},{4,0},{8,12},{12,8},{16,20},{20,16},{24,28},{28,24},{1,5},{5... | collective-permute-start | bytes 3538952 | tf_op jit(solution)/shard_map/ppermute | solution.py:255
  149.4 26.4 %collective-permute-start.13 = (bf16[4,64,1152]{2,1,0:T(8,128)(2,1)}, bf16[4,64,1152]{2,1,0:T(8,128)(2,1)S(1)}, u32[]{:S(2)}, u32[]{:S(2)}) collective-permute-start(bf16[4,64,1152]{2,1,0:T(8,128)(2,1)} %select_convert_fusion.1), channel_id=1, source_target_pairs={{0,8},{4,12},{8,0},{12,4},{16,24},{20,28},{24,16},{28,20},{1,9},{5... | collective-permute-start | bytes 1769480 | tf_op jit(solution)/shard_map/ppermute | solution.py:255
  176.0 8.8 %collective-permute-start.14 = (bf16[4,32,1152]{2,1,0:T(8,128)(2,1)S(1)}, bf16[4,32,1152]{2,1,0:T(8,128)(2,1)S(1)}, u32[]{:S(2)}, u32[]{:S(2)}) collective-permute-start(bf16[4,32,1152]{2,1,0:T(8,128)(2,1)S(1)} %select_convert_fusion.2), channel_id=1, source_target_pairs={{0,16},{4,20},{8,24},{12,28},{16,0},{20,4},{24,8},{28,12},{1,17},{... | collective-permute-start | bytes 884744 | tf_op jit(solution)/shard_map/ppermute | solution.py:255
  184.9 22.6 %copy-start.12 = (bf16[512,512]{1,0:T(8,128)(2,1)S(1)}, bf16[512,512]{1,0:T(8,128)(2,1)}, u32[]{:S(2)}) copy-start(bf16[512,512]{1,0:T(8,128)(2,1)} %copy-done.10) | copy-start | bytes 1572868
  184.9 22.6 %copy-start.20 = (f32[768,512]{1,0:T(8,128)S(1)}, f32[768,512]{1,0:T(8,128)}, u32[]{:S(2)}) copy-start(f32[768,512]{1,0:T(8,128)} %copy-done.19) | copy-start | bytes 4718596
  184.9 10.2 %collective-permute-start.15 = (bf16[32,1152]{1,0:T(8,128)(2,1)S(1)}, bf16[32,1152]{1,0:T(8,128)(2,1)S(1)}, u32[]{:S(2)}, u32[]{:S(2)}) collective-permute-start(bf16[32,1152]{1,0:T(8,128)(2,1)S(1)} %get-tuple-element.50), channel_id=1, source_target_pairs={{0,1},{1,2},{2,3},{3,0},{4,5},{5,6},{6,7},{7,4},{8,9},{9,10},{10,1... | collective-permute-start | bytes 221192 | tf_op jit(solution)/shard_map/ppermute | solution.py:286
  190.1 7.3 %collective-permute-start.16 = (bf16[32,1152]{1,0:T(8,128)(2,1)S(1)}, bf16[32,1152]{1,0:T(8,128)(2,1)S(1)}, u32[]{:S(2)}, u32[]{:S(2)}) collective-permute-start(bf16[32,1152]{1,0:T(8,128)(2,1)S(1)} %get-tuple-element.52), channel_id=1, source_target_pairs={{0,2},{1,3},{2,0},{3,1},{4,6},{5,7},{6,4},{7,5},{8,10},{9,11},{10,... | collective-permute-start | bytes 221192 | tf_op jit(solution)/shard_map/ppermute | solution.py:286
  192.7 4.9 %collective-permute-start.17 = (bf16[32,1152]{1,0:T(8,128)(2,1)S(1)}, bf16[32,1152]{1,0:T(8,128)(2,1)S(1)}, u32[]{:S(2)}, u32[]{:S(2)}) collective-permute-start(bf16[32,1152]{1,0:T(8,128)(2,1)S(1)} %get-tuple-element.51), channel_id=1, source_target_pairs={{0,3},{1,0},{2,1},{3,2},{4,7},{5,4},{6,5},{7,6},{8,11},{9,8},{10,9... | collective-permute-start | bytes 221192 | tf_op jit(solution)/shard_map/ppermute | solution.py:286
  197.6 4.4 %collective-permute-start.18 = (bf16[32,1152]{1,0:T(8,128)(2,1)S(1)}, bf16[32,1152]{1,0:T(8,128)(2,1)S(1)}, u32[]{:S(2)}, u32[]{:S(2)}) collective-permute-start(bf16[32,1152]{1,0:T(8,128)(2,1)S(1)} %fusion.32), channel_id=1, source_target_pairs={{0,16},{4,20},{8,24},{12,28},{16,0},{20,4},{24,8},{28,12},{1,17},{... | collective-permute-start | bytes 221192 | tf_op jit(solution)/shard_map/ppermute | solution.py:255
  202.1 5.8 %copy-start.23 = (bf16[384,512]{1,0:T(8,128)(2,1)S(1)}, bf16[384,512]{1,0:T(8,128)(2,1)}, u32[]{:S(2)}) copy-start(bf16[384,512]{1,0:T(8,128)(2,1)} %get-tuple-element.43) | copy-start | bytes 1179652
  202.1 5.2 %collective-permute-start.19 = (bf16[64,1152]{1,0:T(8,128)(2,1)S(1)}, bf16[64,1152]{1,0:T(8,128)(2,1)S(1)}, u32[]{:S(2)}, u32[]{:S(2)}) collective-permute-start(bf16[64,1152]{1,0:T(8,128)(2,1)S(1)} %pad_maximum_fusion.6), channel_id=1, source_target_pairs={{0,8},{4,12},{8,0},{12,4},{16,24},{20,28},{24,16},{28,20},{1,9},{5... | collective-permute-start | bytes 442376 | tf_op jit(solution)/shard_map/ppermute | solution.py:255
  207.4 1.6 collective-permute-start.20
  209.2 6.9 %collective-permute-start.21 = (bf16[256,128]{1,0:T(8,128)(2,1)S(1)}, bf16[256,128]{1,0:T(8,128)(2,1)S(1)}, u32[]{:S(2)}, u32[]{:S(2)}) collective-permute-start(bf16[256,128]{1,0:T(8,128)(2,1)S(1)} %get-tuple-element.29), channel_id=1, source_target_pairs={{0,1},{1,2},{2,3},{3,0},{4,5},{5,6},{6,7},{7,4},{8,9},{9,10},{10,1... | collective-permute-start | bytes 196616 | tf_op jit(solution)/shard_map/ppermute | solution.py:249
  210.5 7.8 %collective-permute-start.22 = (bf16[256,128]{1,0:T(8,128)(2,1)S(1)}, bf16[256,128]{1,0:T(8,128)(2,1)S(1)}, u32[]{:S(2)}, u32[]{:S(2)}) collective-permute-start(bf16[256,128]{1,0:T(8,128)(2,1)S(1)} %get-tuple-element.29), channel_id=1, source_target_pairs={{0,2},{1,3},{2,0},{3,1},{4,6},{5,7},{6,4},{7,5},{8,10},{9,11},{10,... | collective-permute-start | bytes 196616 | tf_op jit(solution)/shard_map/ppermute | solution.py:249
  212.4 6.1 %collective-permute-start.23 = (bf16[256,128]{1,0:T(8,128)(2,1)S(1)}, bf16[256,128]{1,0:T(8,128)(2,1)S(1)}, u32[]{:S(2)}, u32[]{:S(2)}) collective-permute-start(bf16[256,128]{1,0:T(8,128)(2,1)S(1)} %get-tuple-element.29), channel_id=1, source_target_pairs={{0,3},{1,0},{2,1},{3,2},{4,7},{5,4},{6,5},{7,6},{8,11},{9,8},{10,9... | collective-permute-start | bytes 196616 | tf_op jit(solution)/shard_map/ppermute | solution.py:249
